TPU v7x, 128 devices: a whole 4x4x4 slice. The times are simulated.
128 devices in a mesh: dp: 4 (over x), expert: 32 (over z, y, core).
Axes of the slice: x: 4, y: 4, z: 4, core: 2. Of those that a mesh axis runs over, the one named last changes fastest.
Arguments:
- tokens: bfloat16 [16384, 2048], P(('dp', 'expert')), may hold values from -24 to 24
- expert_ids: int32 [16384, 4], P(('dp', 'expert')), may hold values from 0 to 63, all different within a row; in each aligned block of 128 rows (0 to 127, 128 to 255, ...) at most 16 rows name the same one
- gate_probs: float32 [16384, 4], P(('dp', 'expert')), may hold values from 0.05 to 1
- w_gate: bfloat16 [64, 2048, 768], P('expert'), may hold values from -0.125 to 0.125
- w_up: bfloat16 [64, 2048, 768], P('expert'), may hold values from -0.125 to 0.125
- w_down: bfloat16 [64, 768, 2048], P('expert'), may hold values from -0.21875 to 0.21875
- out_grad: bfloat16 [16384, 2048], P(('dp', 'expert')), may hold values from -24 to 24
Outputs:
- layer_out: bfloat16 [16384, 2048], P(('dp', 'expert'))
- token_grad: bfloat16 [16384, 2048], P(('dp', 'expert'))
- gate_grad: float32 [16384, 4], P(('dp', 'expert'))
- grad_gate: float32 [64, 2048, 768], P('expert', 'dp')
- grad_up: float32 [64, 2048, 768], P('expert', 'dp')
- grad_down: float32 [64, 768, 2048], P('expert', None, 'dp')
Inputs may be any that keep to these rules, and one draw needn't show every extreme that they name: `expert_ids`: each token names 4 different experts. In each aligned block of 128 rows (the tokens of one device) no expert is named by more than 16 rows, a bound that some block reaches.
All inputs are finite; a program needn't handle non-finite values.
Results may differ from a plain program's by a relative error of at most 0.012.
Values may be sent and summed in bfloat16 or wider, within the bound.
A program may use at most 192 MiB of HBM per device.

v0:
```python
import jax
import jax.numpy as jnp
from jax import lax
from jax.sharding import PartitionSpec as P


def silu_parts(pre_value):
    logistic = 1.0 / (1.0 + jnp.exp(-pre_value))
    return (pre_value * logistic, logistic)


def slot_layout(expert_ids, local_count, owners, capacity):
    tok_dev, choose = expert_ids.shape
    flat_ids = expert_ids.reshape(tok_dev * choose)
    one_hot = (
        flat_ids[:, None] == jnp.arange(local_count * owners, dtype=jnp.int32)[None, :]
    ).astype(jnp.int32)
    rank_in = jnp.sum((jnp.cumsum(one_hot, axis=0) - 1) * one_hot, axis=1)
    owner_idx = flat_ids // local_count
    local_idx = flat_ids % local_count
    return (local_idx * owners + owner_idx) * capacity + rank_in


def shards(tokens, expert_ids, gate_probs, w_gate, w_up, w_down, out_grad):
    tok_dev, choose = expert_ids.shape
    features = tokens.shape[1]
    local_count = w_gate.shape[0]
    owners = lax.axis_size("expert")
    capacity = min(tok_dev, 2 * tok_dev * choose // (local_count * owners))
    row_count = tok_dev * choose
    slot_count = local_count * owners * capacity
    group_rows = owners * capacity
    slot_index = slot_layout(expert_ids, local_count, owners, capacity)
    source = (
        jnp.full((slot_count,), row_count, jnp.int32)
        .at[slot_index]
        .set(jnp.arange(row_count, dtype=jnp.int32))
    )
    is_used = source < row_count
    tok_index = jnp.where(is_used, source // choose, tok_dev)
    zero_row = jnp.zeros((1, features), jnp.bfloat16)
    send_tokens = jnp.concatenate([tokens, zero_row], axis=0)[tok_index].reshape(
        local_count, owners, capacity, features
    )
    prob_slot = jnp.where(
        is_used, gate_probs.reshape(row_count)[jnp.minimum(source, row_count - 1)], 0.0
    )
    grad_rows = jnp.concatenate([out_grad, zero_row], axis=0)[tok_index]
    send_delta = (
        (prob_slot[:, None] * grad_rows)
        .astype(jnp.bfloat16)
        .reshape(local_count, owners, capacity, features)
    )
    recv_tokens = lax.all_to_all(send_tokens, "expert", split_axis=1, concat_axis=1, tiled=True)
    recv_tokens = recv_tokens.reshape(local_count, group_rows, features)
    pre_gate = jnp.einsum("esd,edf->esf", recv_tokens, w_gate, preferred_element_type=jnp.float32)
    pre_up = jnp.einsum("esd,edf->esf", recv_tokens, w_up, preferred_element_type=jnp.float32)
    activated, logistic = silu_parts(pre_gate)
    act = (activated * pre_up).astype(jnp.bfloat16)
    expert_out = jnp.einsum("esf,efd->esd", act, w_down, preferred_element_type=jnp.float32).astype(
        jnp.bfloat16
    )
    returned = lax.all_to_all(
        expert_out.reshape(local_count, owners, capacity, features),
        "expert",
        split_axis=1,
        concat_axis=1,
        tiled=True,
    )
    out_rows = returned.reshape(slot_count, features)[slot_index].reshape(tok_dev, choose, features)
    layer_out = jnp.sum(gate_probs[:, :, None] * out_rows, axis=1).astype(jnp.bfloat16)
    gate_grad = jnp.einsum("tkd,td->tk", out_rows, out_grad, preferred_element_type=jnp.float32)
    recv_delta = lax.all_to_all(send_delta, "expert", split_axis=1, concat_axis=1, tiled=True)
    recv_delta = recv_delta.reshape(local_count, group_rows, features)
    act_delta = jnp.einsum("esd,efd->esf", recv_delta, w_down, preferred_element_type=jnp.float32)
    gate_delta = (act_delta * pre_up * logistic * (1.0 + pre_gate * (1.0 - logistic))).astype(
        jnp.bfloat16
    )
    up_delta = (act_delta * activated).astype(jnp.bfloat16)
    row_grad = (
        jnp.einsum("esf,edf->esd", gate_delta, w_gate, preferred_element_type=jnp.float32)
        + jnp.einsum("esf,edf->esd", up_delta, w_up, preferred_element_type=jnp.float32)
    ).astype(jnp.bfloat16)
    back_rows = lax.all_to_all(
        row_grad.reshape(local_count, owners, capacity, features),
        "expert",
        split_axis=1,
        concat_axis=1,
        tiled=True,
    )
    token_rows = back_rows.reshape(slot_count, features)[slot_index].reshape(
        tok_dev, choose, features
    )
    token_grad = jnp.sum(token_rows.astype(jnp.float32), axis=1).astype(jnp.bfloat16)
    gate_part = jnp.einsum(
        "esd,esf->edf", recv_tokens, gate_delta, preferred_element_type=jnp.float32
    )
    up_part = jnp.einsum("esd,esf->edf", recv_tokens, up_delta, preferred_element_type=jnp.float32)
    down_turned = jnp.einsum("esd,esf->edf", recv_delta, act, preferred_element_type=jnp.float32)
    grad_gate, grad_up, down_share = (
        lax.psum_scatter(
            gate_part.astype(jnp.bfloat16), "dp", scatter_dimension=1, tiled=True
        ).astype(jnp.float32),
        lax.psum_scatter(
            up_part.astype(jnp.bfloat16), "dp", scatter_dimension=1, tiled=True
        ).astype(jnp.float32),
        lax.psum_scatter(
            down_turned.astype(jnp.bfloat16), "dp", scatter_dimension=1, tiled=True
        ).astype(jnp.float32),
    )
    grad_down = jnp.swapaxes(down_share, 1, 2)
    return (layer_out, token_grad, gate_grad, grad_gate, grad_up, grad_down)


def solution(mesh):
    in_specs = (
        P(("dp", "expert"), None),
        P(("dp", "expert"), None),
        P(("dp", "expert"), None),
        P("expert", None, None),
        P("expert", None, None),
        P("expert", None, None),
        P(("dp", "expert"), None),
    )
    out_specs = (
        P(("dp", "expert"), None),
        P(("dp", "expert"), None),
        P(("dp", "expert"), None),
        P("expert", "dp", None),
        P("expert", "dp", None),
        P("expert", None, "dp"),
    )
    return jax.shard_map(shards, mesh=mesh, in_specs=in_specs, out_specs=out_specs, check_vma=False)
```

profile of v0, /device:TPU:1, one launch (start us, length us, event | category | flops | bytes accessed | tf_op | source)
XLA Modules:
  0.0 367.7 jit_solution(10526601077468934454)
XLA Ops:
  7.2 0.8 copy.29
  8.3 1.2 reduce-window.6
  9.9 2.4 scatter_custom_fusion
  12.4 1.1 concatenate.6
  13.5 6.0 %gather_fusion = bf16[1024,2048]{1,0:T(8,128)(2,1)} fusion(bf16[129,2048]{1,0:T(8,128)(2,1)S(1)} %concatenate.6, s32[1024]{0:T(1024)S(1)} %get-tuple-element.28), kind=kCustom, calls=%fused_computation | custom fusion | bytes 8392704 | tf_op jit(solution)/shard_map/gather | solution.py:42
  19.5 4.7 %copy.33 = bf16[2,32,16,2048]{3,2,0,1:T(8,128)(2,1)} copy(bf16[2,32,16,2048]{3,2,1,0:T(8,128)(2,1)} %bitcast.53) | data formatting | bytes 8388608 | tf_op jit(solution)/shard_map/reshape | solution.py:42
  24.3 9.8 %all-to-all-start = ((bf16[2,32,16,2048]{3,2,0,1:T(8,128)(2,1)}), bf16[2,32,16,2048]{3,2,0,1:T(8,128)(2,1)}, u32[]{:S(2)}, u32[]{:S(2)}) async-start(bf16[2,32,16,2048]{3,2,0,1:T(8,128)(2,1)} %copy.33), calls=%async_computation | async-start | bytes 8388608 | tf_op jit(solution)/shard_map/all_to_all | solution.py:54
  34.3 6.9 %gather_fusion.2 = f32[1024]{0:T(1024)S(1)} fusion(f32[512]{0:T(512)S(1)} %reshape.202, s32[1024]{0:T(1024)S(1)} %get-tuple-element.27), kind=kCustom, calls=%fused_computation.2 | custom fusion | bytes 12288 | tf_op jit(solution)/shard_map/gather | solution.py:46
  41.4 6.0 %gather_fusion.3 = bf16[1024,2048]{1,0:T(8,128)(2,1)} fusion(bf16[129,2048]{1,0:T(8,128)(2,1)S(1)} %concatenate.7, s32[1024]{0:T(1024)S(1)} %get-tuple-element.28), kind=kCustom, calls=%fused_computation.3 | custom fusion | bytes 8392704 | tf_op jit(solution)/shard_map/gather | solution.py:48
  47.4 4.9 %fusion = bf16[2,32,16,2048]{3,2,0,1:T(8,128)(2,1)} fusion(f32[2,32,16]{2,0,1:T(2,128)S(1)} %copy.38, bf16[2,32,16,2048]{3,2,1,0:T(8,128)(2,1)} %bitcast.52), kind=kLoop, calls=%fused_computation.7 | loop fusion | flops 6291456 | bytes 8392704 | tf_op jit(solution)/shard_map/convert_element_type | solution.py:51
  52.3 32.0 %all-to-all-done = bf16[2,32,16,2048]{3,2,0,1:T(8,128)(2,1)} async-done(((bf16[2,32,16,2048]{3,2,0,1:T(8,128)(2,1)}), bf16[2,32,16,2048]{3,2,0,1:T(8,128)(2,1)}, u32[]{:S(2)}, u32[]{:S(2)}) %all-to-all-start) | async-done | bytes 4194336 | tf_op jit(solution)/shard_map/all_to_all | solution.py:54
  84.3 8.0 %all-to-all-start.2 = ((bf16[2,32,16,2048]{3,2,0,1:T(8,128)(2,1)}), bf16[2,32,16,2048]{3,2,0,1:T(8,128)(2,1)}, u32[]{:S(2)}, u32[]{:S(2)}) async-start(bf16[2,32,16,2048]{3,2,0,1:T(8,128)(2,1)} %fusion), calls=%async_computation.2 | async-start | bytes 8388608 | tf_op jit(solution)/shard_map/all_to_all | solution.py:73
  92.3 0.6 reduce-scatter.8.cloned.1.call-start
  92.9 2.7 copy.34
  95.6 9.5 %fusion.17 = f32[2,512,768]{2,1,0:T(8,128)} fusion(bf16[2,512,2048]{2,1,0:T(8,128)(2,1)S(1)} %bitcast.54, bf16[2,2048,768]{2,1,0:T(8,128)(2,1)} %param.11), kind=kOutput, calls=%fused_computation.56 | convolution fusion | flops 3221225472 | bytes 13631488 | tf_op jit(solution)/shard_map/esd,edf->esf/dot_general | solution.py:57
  105.1 5.1 %fusion.16 = f32[2,512,768]{2,1,0:T(8,128)} fusion(bf16[2,512,2048]{2,1,0:T(8,128)(2,1)S(1)} %bitcast.55, bf16[2,2048,768]{2,1,0:T(8,128)(2,1)S(1)} %bitcast.68), kind=kOutput, calls=%fused_computation.55 | convolution fusion | flops 3221225472 | bytes 13631488 | tf_op jit(solution)/shard_map/esd,edf->esf/dot_general | solution.py:56
  110.2 32.5 %all-to-all-done.2 = bf16[2,32,16,2048]{3,2,0,1:T(8,128)(2,1)} async-done(((bf16[2,32,16,2048]{3,2,0,1:T(8,128)(2,1)}), bf16[2,32,16,2048]{3,2,0,1:T(8,128)(2,1)}, u32[]{:S(2)}, u32[]{:S(2)}) %all-to-all-start.2) | async-done | bytes 4194336 | tf_op jit(solution)/shard_map/all_to_all | solution.py:73
  142.7 2.7 copy.40
  145.3 0.5 copy-done.5
  145.8 9.2 %multiply_convert_fusion = (bf16[2,512,768]{2,1,0:T(8,128)(2,1)}, bf16[2,512,768]{2,1,0:T(8,128)(2,1)}, bf16[2,512,768]{2,1,0:T(8,128)(2,1)S(1)}) fusion(f32[2,512,768]{2,1,0:T(8,128)} %fusion.16, f32[2,512,768]{2,1,0:T(8,128)S(1)} %copy-done.5, bf16[2,512,2048]{2,1,0:T(8,128)(2,1)S(1)} %bitcast.58, bf16[2,768,2048]{2,1,0:T(8,128)(2,1)} %param.12), kind=kOutput, calls=%fused_computation.15 | convolution fusion | flops 3233021952 | bytes 21495808 | tf_op jit(solution)/shard_map/esd,efd->esf/dot_general | solution.py:75
  155.0 1.1 copy-done.4
  156.2 5.4 %convolution_convert_fusion = bf16[2,2048,768]{2,1,0:T(8,128)(2,1)} fusion(bf16[2,512,2048]{2,1,0:T(8,128)(2,1)S(1)} %bitcast.59, bf16[2,512,768]{2,1,0:T(8,128)(2,1)S(1)} %get-tuple-element.26), kind=kOutput, calls=%fused_computation.9 | convolution fusion | flops 3224371200 | bytes 12058624 | tf_op jit(solution)/shard_map/esd,esf->edf/dot_general | solution.py:99
  161.8 9.0 %convolution_convert_fusion.1 = bf16[2,2048,768]{2,1,0:T(8,128)(2,1)} fusion(bf16[2,512,2048]{2,1,0:T(8,128)(2,1)} %bitcast.56, bf16[2,512,768]{2,1,0:T(8,128)(2,1)} %get-tuple-element.24), kind=kOutput, calls=%fused_computation.10 | convolution fusion | flops 3224371200 | bytes 12058624 | tf_op jit(solution)/shard_map/esd,esf->edf/dot_general | solution.py:98
  170.9 9.2 %convolution_convert_fusion.2 = bf16[2,2048,768]{2,1,0:T(8,128)(2,1)} fusion(bf16[2,512,2048]{2,1,0:T(8,128)(2,1)} %bitcast.57, bf16[2,512,768]{2,1,0:T(8,128)(2,1)} %get-tuple-element.25), kind=kOutput, calls=%fused_computation.11 | convolution fusion | flops 3224371200 | bytes 12058624 | tf_op jit(solution)/shard_map/esd,esf->edf/dot_general | solution.py:95
  180.1 6.7 %convolution_convert_fusion.3 = bf16[2,512,2048]{2,1,0:T(8,128)(2,1)S(1)} fusion(bf16[2,512,768]{2,1,0:T(8,128)(2,1)} %copy-done.4, bf16[2,768,2048]{2,1,0:T(8,128)(2,1)} %param.12), kind=kOutput, calls=%fused_computation.13 | convolution fusion | flops 3223322624 | bytes 12058624 | tf_op jit(solution)/shard_map/esf,efd->esd/dot_general | solution.py:60
  186.8 2.3 copy.35
  189.1 7.9 %all-to-all-start.1 = ((bf16[2,32,16,2048]{3,2,0,1:T(8,128)(2,1)}), bf16[2,32,16,2048]{3,2,0,1:T(8,128)(2,1)}, u32[]{:S(2)}, u32[]{:S(2)}) async-start(bf16[2,32,16,2048]{3,2,0,1:T(8,128)(2,1)} %copy.35), calls=%async_computation.1 | async-start | bytes 8388608 | tf_op jit(solution)/shard_map/all_to_all | solution.py:63
  197.0 10.1 %fusion.18 = f32[2,512,2048]{2,1,0:T(8,128)} fusion(bf16[2,512,768]{2,1,0:T(8,128)(2,1)} %get-tuple-element.25, bf16[2,2048,768]{2,1,0:T(8,128)(2,1)} %param.10), kind=kOutput, calls=%fused_computation.57 | convolution fusion | flops 3221225472 | bytes 16252928 | tf_op jit(solution)/shard_map/esf,edf->esd/dot_general | solution.py:81
  207.1 7.8 %add_convert_fusion = bf16[2,512,2048]{2,1,0:T(8,128)(2,1)S(1)} fusion(f32[2,512,2048]{2,1,0:T(8,128)} %fusion.18, bf16[2,512,768]{2,1,0:T(8,128)(2,1)S(1)} %copy-done.3, bf16[2,2048,768]{2,1,0:T(8,128)(2,1)} %param.11), kind=kOutput, calls=%fused_computation.8 | convolution fusion | flops 3225419776 | bytes 20447232 | tf_op jit(solution)/shard_map/esf,edf->esd/dot_general | solution.py:82
  214.9 2.6 copy.41
  217.4 29.7 %all-to-all-done.1 = bf16[2,32,16,2048]{3,2,0,1:T(8,128)(2,1)} async-done(((bf16[2,32,16,2048]{3,2,0,1:T(8,128)(2,1)}), bf16[2,32,16,2048]{3,2,0,1:T(8,128)(2,1)}, u32[]{:S(2)}, u32[]{:S(2)}) %all-to-all-start.1) | async-done | bytes 4194336 | tf_op jit(solution)/shard_map/all_to_all | solution.py:63
  247.1 8.0 %all-to-all-start.3 = ((bf16[2,32,16,2048]{3,2,0,1:T(8,128)(2,1)}), bf16[2,32,16,2048]{3,2,0,1:T(8,128)(2,1)}, u32[]{:S(2)}, u32[]{:S(2)}) async-start(bf16[2,32,16,2048]{3,2,0,1:T(8,128)(2,1)} %copy.41), calls=%async_computation.3 | async-start | bytes 8388608 | tf_op jit(solution)/shard_map/all_to_all | solution.py:84
  255.1 4.7 %copy.36 = bf16[2,32,16,2048]{3,2,1,0:T(8,128)(2,1)} copy(bf16[2,32,16,2048]{3,2,0,1:T(8,128)(2,1)} %all-to-all-done.1) | data formatting | bytes 8388608 | tf_op jit(solution)/shard_map/all_to_all | solution.py:63
  259.9 7.1 %gather_fusion.1 = bf16[512,2048]{1,0:T(8,128)(2,1)S(1)} fusion(bf16[1024,2048]{1,0:T(8,128)(2,1)} %bitcast.51, s32[1024]{0:T(1024)S(1)} %pad_clamp_fusion), kind=kCustom, calls=%fused_computation.1 | custom fusion | bytes 4196352 | tf_op jit(solution)/shard_map/gather | solution.py:70
  267.0 2.2 reshape.201
  269.2 4.5 %fusion.2 = f32[128,1,4]{2,1,0:T(1,128)S(1)} fusion(bf16[128,4,2048]{2,1,0:T(4,128)(2,1)} %reshape.201, bf16[128,2048,1]{1,0,2:T(8,128)(2,1)S(1)} %bitcast.62), kind=kOutput, calls=%fused_computation.20 | convolution fusion | flops 2097152 | bytes 2623488 | tf_op jit(solution)/shard_map/tkd,td->tk/dot_general | solution.py:72
  273.7 0.7 copy.48
  274.4 31.1 %all-to-all-done.3 = bf16[2,32,16,2048]{3,2,0,1:T(8,128)(2,1)} async-done(((bf16[2,32,16,2048]{3,2,0,1:T(8,128)(2,1)}), bf16[2,32,16,2048]{3,2,0,1:T(8,128)(2,1)}, u32[]{:S(2)}, u32[]{:S(2)}) %all-to-all-start.3) | async-done | bytes 4194336 | tf_op jit(solution)/shard_map/all_to_all | solution.py:84
  305.5 4.7 %copy.42 = bf16[2,32,16,2048]{3,2,1,0:T(8,128)(2,1)} copy(bf16[2,32,16,2048]{3,2,0,1:T(8,128)(2,1)} %all-to-all-done.3) | data formatting | bytes 8388608 | tf_op jit(solution)/shard_map/all_to_all | solution.py:84
  310.3 7.3 %gather_fusion.4 = bf16[512,2048]{1,0:T(8,128)(2,1)S(1)} fusion(bf16[1024,2048]{1,0:T(8,128)(2,1)} %bitcast.50, s32[1024]{0:T(1024)S(1)} %pad_clamp_fusion), kind=kCustom, calls=%fused_computation.4 | custom fusion | bytes 4196352 | tf_op jit(solution)/shard_map/gather | solution.py:91
  317.5 2.4 reshape.206
  320.0 5.0 %reduce_sum.35 = bf16[128,2048]{1,0:T(8,128)(2,1)} reduce(bf16[128,4,2048]{2,1,0:T(4,128)(2,1)} %reshape.206, bf16[]{:T(256)} %constant.53.clone.1), dimensions={1}, to_apply=%region_5.6 | reduce | flops 786432 | bytes 2621442 | tf_op jit(solution)/shard_map/reduce_sum | solution.py:94
  324.9 5.7 %multiply_reduce_fusion = bf16[128,2048]{1,0:T(8,128)(2,1)} fusion(bf16[128,4,2048]{2,1,0:T(4,128)(2,1)} %reshape.201, f32[128,4]{1,0:T(8,128)S(1)} %copy.28), kind=kLoop, calls=%fused_computation.12 | loop fusion | flops 2883584 | bytes 2623488 | tf_op jit(solution)/shard_map/reduce_sum | solution.py:71
  330.6 1.6 convert_bitcast_fusion
  332.3 2.4 copy.46
  334.6 3.3 convert_element_type.69
  337.9 19.7 %reduce-scatter.4.cloned.1.call-done = bf16[2,512,768]{2,1,0:T(8,128)(2,1)} async-done(((bf16[2,2048,768]{2,1,0:T(8,128)(2,1)}), bf16[2,512,768]{2,1,0:T(8,128)(2,1)}) %reduce-scatter.4.cloned.1.call-update) | async-done | bytes 1572880 | tf_op jit(solution)/shard_map/reduce_scatter | solution.py:101
  357.6 3.3 convert_element_type.67
  (40 shorter events, 1.5 us)
Async XLA Ops:
  24.3 9.8 %copy-start.2 = (f32[128,4]{0,1:T(4,128)S(1)}, f32[128,4]{0,1:T(4,128)}, u32[]{:S(2)}) copy-start(f32[128,4]{0,1:T(4,128)} %param.9) | copy-start | bytes 6148
  24.3 60.1 %all-to-all-start = ((bf16[2,32,16,2048]{3,2,0,1:T(8,128)(2,1)}), bf16[2,32,16,2048]{3,2,0,1:T(8,128)(2,1)}, u32[]{:S(2)}, u32[]{:S(2)}) async-start(bf16[2,32,16,2048]{3,2,0,1:T(8,128)(2,1)} %copy.33), calls=%async_computation | async-start | bytes 8388608 | tf_op jit(solution)/shard_map/all_to_all | solution.py:54
  34.1 7.2 %copy-start.1 = (bf16[128,2048]{1,0:T(8,128)(2,1)S(1)}, bf16[128,2048]{1,0:T(8,128)(2,1)}, u32[]{:S(2)}) copy-start(bf16[128,2048]{1,0:T(8,128)(2,1)} %param.13) | copy-start | bytes 1572868
  84.3 58.4 %all-to-all-start.2 = ((bf16[2,32,16,2048]{3,2,0,1:T(8,128)(2,1)}), bf16[2,32,16,2048]{3,2,0,1:T(8,128)(2,1)}, u32[]{:S(2)}, u32[]{:S(2)}) async-start(bf16[2,32,16,2048]{3,2,0,1:T(8,128)(2,1)} %fusion), calls=%async_computation.2 | async-start | bytes 8388608 | tf_op jit(solution)/shard_map/all_to_all | solution.py:73
  92.3 238.3 %reduce-scatter.8.cloned.1.call-start = ((), (), s32[]{:S(2)}) async-start(), calls=%async_computation.9 | async-start | bytes 7864320 | tf_op jit(solution)/shard_map/reduce_scatter | solution.py:107
  92.9 12.2 %slice-start = ((s8[6291456]{0:T(1024)(128)(4,1)}), s8[4194304]{0:T(1024)(128)(4,1)S(1)}, s32[]{:S(2)}) async-start(s8[6291456]{0:T(1024)(128)(4,1)} %bitcast.67), calls=%async_computation.10 | async-start | bytes 8388608
  95.5 9.5 %copy-start = (bf16[2,32,16,2048]{3,2,1,0:T(8,128)(2,1)}, bf16[2,32,16,2048]{3,2,1,0:T(8,128)(2,1)S(1)}, u32[]{:S(2)}) copy-start(bf16[2,32,16,2048]{3,2,1,0:T(8,128)(2,1)S(1)} %copy.34) | copy-start | bytes 12582916
  95.6 9.5 %slice-start.1 = ((s8[6291456]{0:T(1024)(128)(4,1)}), s8[2097152]{0:T(1024)(128)(4,1)S(1)}, s32[]{:S(2)}) async-start(s8[6291456]{0:T(1024)(128)(4,1)} %bitcast.67), calls=%async_computation.11 | async-start | bytes 4194304
  142.7 3.2 copy-start.5
  155.0 1.1 copy-start.4
  161.6 173.0 %reduce-scatter.6.cloned.1.call-start = ((), (), s32[]{:S(2)}) async-start(), calls=%async_computation.8 | async-start | bytes 7864320 | tf_op jit(solution)/shard_map/reduce_scatter | solution.py:104
  170.8 186.8 %reduce-scatter.4.cloned.1.call-start = ((), (), s32[]{:S(2)}) async-start(), calls=%async_computation.7 | async-start | bytes 7864320 | tf_op jit(solution)/shard_map/reduce_scatter | solution.py:101
  189.1 58.0 %all-to-all-start.1 = ((bf16[2,32,16,2048]{3,2,0,1:T(8,128)(2,1)}), bf16[2,32,16,2048]{3,2,0,1:T(8,128)(2,1)}, u32[]{:S(2)}, u32[]{:S(2)}) async-start(bf16[2,32,16,2048]{3,2,0,1:T(8,128)(2,1)} %copy.35), calls=%async_computation.1 | async-start | bytes 8388608 | tf_op jit(solution)/shard_map/all_to_all | solution.py:63
  197.0 10.1 %copy-start.3 = (bf16[2,512,768]{2,1,0:T(8,128)(2,1)S(1)}, bf16[2,512,768]{2,1,0:T(8,128)(2,1)}, u32[]{:S(2)}) copy-start(bf16[2,512,768]{2,1,0:T(8,128)(2,1)} %get-tuple-element.24) | copy-start | bytes 4718596
  247.1 58.4 %all-to-all-start.3 = ((bf16[2,32,16,2048]{3,2,0,1:T(8,128)(2,1)}), bf16[2,32,16,2048]{3,2,0,1:T(8,128)(2,1)}, u32[]{:S(2)}, u32[]{:S(2)}) async-start(bf16[2,32,16,2048]{3,2,0,1:T(8,128)(2,1)} %copy.41), calls=%async_computation.3 | async-start | bytes 8388608 | tf_op jit(solution)/shard_map/all_to_all | solution.py:84
Sparse Core Ops, SparseCore 0:
  161.7 63.6 reduce-scatter.7
  227.8 63.6 reduce-scatter.5
  293.9 63.6 reduce-scatter.3
where the time goes:
time: 373 us; the launch traced here: 368 us
  waiting for transfers between devices  145 us (39%)
  matrix products  76.4 us (20%)
  local copies, waits for them, and re-layouts  72.2 us (19%)
  starting transfers between devices  34.5 us (9%)
  other arithmetic  25.3 us (7%)
  between operations  14.3 us (4%)
    all_to_all x1, waiting for transfers between devices, shards(): lax.all_to_all(send_delta, 'expert', split_axis=1, concat_axis=1, tiled=T...  32.5 us
    all_to_all x1, waiting for transfers between devices, shards(): lax.all_to_all(send_tokens, 'expert', split_axis=1, concat_axis=1, tiled=...  32 us
    all_to_all x1, waiting for transfers between devices, shards(): lax.all_to_all(row_grad.reshape(local_count, owners, capacity, features),...  31.1 us
    all_to_all x1, waiting for transfers between devices, shards(): lax.all_to_all(expert_out.reshape(local_count, owners, capacity, features...  29.7 us
    reduce_scatter x1, waiting for transfers between devices, shards(): lax.psum_scatter(gate_part.astype(jnp.bfloat16), 'dp', scatter_dimension=...  19.7 us
    dot_general x1, matrix products, shards(): jnp.einsum('esf,edf->esd', gate_delta, w_gate, preferred_element_type=jnp...  10.1 us
    all_to_all x1, starting transfers between devices, shards(): lax.all_to_all(send_tokens, 'expert', split_axis=1, concat_axis=1, tiled=...  9.79 us
    dot_general x1, matrix products, shards(): jnp.einsum('esd,edf->esf', recv_tokens, w_up, preferred_element_type=jnp....  9.46 us
  transfers between devices with their start and end apart: 7, of which 5 were waited for; matrix products, arithmetic and copies ran while one was open for 37% of the time, Pallas kernels for 0%

commit v1 on v0

v1 whole, which is shorter than its diff:
```python
import functools

import jax
import jax.numpy as jnp
from jax import lax
from jax.experimental import pallas as pl
from jax.experimental.pallas import tpu as pltpu
from jax.sharding import PartitionSpec as P

MESH = pl.DeviceIdType.MESH
F32 = jnp.float32
BF16 = jnp.bfloat16
CAP = 16
NT = (((1,), (1,)), ((), ()))
TN = (((0,), (0,)), ((), ()))


def dot(a, b, dims=(((1,), (0,)), ((), ()))):
    return lax.dot_general(a, b, dims, preferred_element_type=F32)


def tiles(count, body):
    if count == 1:
        body(0)
    else:
        lax.fori_loop(0, count, lambda i, c: (body(i), c)[1], 0)


def span(i, size):
    return pl.ds(pl.multiple_of(i * size, size), size)


def kernel(
    n_dp, n_exp,
    route_ref, ids_ref, tok_ref, og_ref, wg_hbm, wu_hbm, wd_hbm,
    lo_ref, tg_ref, gg_ref, own_gu, own_dn, land_gu, land_dn, back,
    send, recv, tt, wg, wu, wd, act, act_t, gd, ud, pre_g, pre_u,
    part_gu, part_dn, mid_gu, mid_dn, sel, sel_t, pslot, acc,
    w_sem, disp_send, disp_recv, back_send, back_recv,
    rs_send, mid_recv, land_sem, own_sem, load_sem,
):
    dp, me = lax.axis_index("dp"), lax.axis_index("expert")
    tok, feats = tok_ref.shape
    hidden = wg.shape[1]
    rows = n_exp * CAP
    top = ids_ref.shape[1]
    right, left = lax.rem(dp + 1, n_dp), lax.rem(dp + n_dp - 1, n_dp)
    across = lax.rem(dp + 2, n_dp)
    f_tile, d_tile = min(256, hidden), min(256, feats)
    n_f, n_d = hidden // f_tile, feats // d_tile
    share = feats // n_dp

    def peer(k):
        if n_exp != 32:
            return lax.rem(me + k, n_exp)
        off = lax.rem(k * 11, 32)
        z, y, c = me // 8, lax.rem(me // 2, 4), lax.rem(me, 2)
        z = lax.rem(z + off // 8, 4)
        y = lax.rem(y + lax.rem(off // 2, 4), 4)
        c = lax.rem(c + lax.rem(off, 2), 2)
        return (z * 4 + y) * 2 + c

    barrier = pltpu.get_barrier_semaphore()

    def greet(k, carry):
        pl.semaphore_signal(barrier, inc=1, device_id={"expert": peer(k)}, device_id_type=MESH)
        return carry

    lax.fori_loop(1, n_exp, greet, 0)
    for side in (left, right):
        pl.semaphore_signal(barrier, inc=1, device_id={"dp": side}, device_id_type=MESH)

    def weights(l):
        return [
            pltpu.make_async_copy(src.at[l], dst, w_sem.at[i])
            for i, (src, dst) in enumerate(((wg_hbm, wg), (wu_hbm, wu), (wd_hbm, wd)))
        ]

    for copy in weights(0):
        copy.start()

    ids_t, probs_t = route_ref[0:top, :], route_ref[top : 2 * top, :]
    earlier = (
        lax.broadcasted_iota(jnp.int32, (tok, tok), 0)
        < lax.broadcasted_iota(jnp.int32, (tok, tok), 1)
    ).astype(F32).astype(BF16)

    def route(l):
        expert = (lax.broadcasted_iota(jnp.int32, (n_exp, tok), 0) * 2 + l).astype(F32)
        named = jnp.zeros((n_exp, tok), F32)
        prob = jnp.zeros((n_exp, tok), F32)
        for k in range(top):
            hit = expert == ids_t[k : k + 1, :]
            named = named + jnp.where(hit, 1.0, 0.0)
            prob = prob + jnp.where(hit, probs_t[k : k + 1, :], 0.0)
        rank = dot(named.astype(BF16), earlier)
        rank = jnp.where(named > 0.0, rank, -1.0)
        slot = lax.broadcasted_iota(jnp.int32, (n_exp, CAP, tok), 1).astype(F32)
        hit = jnp.where(rank[:, None, :] == slot, 1.0, 0.0)
        weight = jnp.sum(hit * prob[:, None, :], axis=2, keepdims=True)
        hit = hit.reshape(rows, tok)
        sel[l] = hit.astype(BF16)
        sel_t[l] = hit.T.astype(BF16)
        pslot[l] = weight.reshape(rows, 1)

    def fill_tokens(l):
        def body(i):
            cols = span(i, d_tile)
            send[2 * l, :, cols] = dot(sel[l], tok_ref[:, cols]).astype(BF16)
        tiles(n_d, body)

    def fill_delta(l):
        def body(i):
            cols = span(i, d_tile)
            send[2 * l + 1, :, cols] = (pslot[l] * dot(sel[l], og_ref[:, cols])).astype(BF16)
        tiles(n_d, body)

    def chunk(i):
        return pl.ds(pl.multiple_of(i * CAP, CAP), CAP)

    def exchange(i, land, send_sem, recv_sem):
        pltpu.make_async_copy(send.at[i, chunk(me)], land.at[i, chunk(me)], recv_sem.at[i]).start()

        def body(k, carry):
            to = peer(k)
            pltpu.make_async_remote_copy(
                src_ref=send.at[i, chunk(to)],
                dst_ref=land.at[i, chunk(me)],
                send_sem=send_sem.at[i],
                recv_sem=recv_sem.at[i],
                device_id={"expert": to},
                device_id_type=MESH,
            ).start()
            return carry

        lax.fori_loop(1, n_exp, body, 0)

    def wait_sent(i, sem):
        part = send.at[i, pl.ds(0, rows - CAP)]
        pltpu.make_async_copy(part, part, sem.at[i]).wait()

    def wait_landed(i, land, sem):
        pltpu.make_async_copy(land.at[i], land.at[i], sem.at[i]).wait()

    def forward(l):
        def body(i):
            cols = span(i, f_tile)
            g = dot(recv[2 * l], wg[:, cols])
            u = dot(recv[2 * l], wu[:, cols])
            pre_g[:, cols] = g
            pre_u[:, cols] = u
            a = (g * (1.0 / (1.0 + jnp.exp(-g))) * u).astype(BF16)
            act[:, cols] = a
            act_t[cols, :] = a.T
        tiles(n_f, body)

    def turn_tokens(l):
        def body(i):
            cols = span(i, d_tile)
            tt[cols, :] = recv[2 * l, :, cols].T
        tiles(n_d, body)

    def outputs(l):
        def body(i):
            cols = span(i, d_tile)
            send[2 * l, :, cols] = dot(act[...], wd[:, cols]).astype(BF16)
        tiles(n_d, body)

    def deltas(l):
        def body(i):
            cols = span(i, f_tile)
            ad = dot(recv[2 * l + 1], wd[cols, :], NT)
            g, u = pre_g[:, cols], pre_u[:, cols]
            s = 1.0 / (1.0 + jnp.exp(-g))
            gd[:, cols] = (ad * u * s * (1.0 + g * (1.0 - s))).astype(BF16)
            ud[:, cols] = (ad * (g * s)).astype(BF16)
        tiles(n_f, body)

    def input_grads(l):
        def body(i):
            cols = span(i, d_tile)
            send[2 * l + 1, :, cols] = (
                dot(gd[...], wg[cols, :], NT) + dot(ud[...], wu[cols, :], NT)
            ).astype(BF16)
        tiles(n_d, body)

    def down_part(l):
        def body(j):
            part_dn[l, j] = dot(act_t[...], recv[2 * l + 1, :, span(j, share)]).astype(BF16)
        tiles(n_dp, body)

    def gate_up_part(l, which):
        src = (gd, ud)[which]

        def body(j):
            part_gu[l, which, j] = dot(tt[span(j, share), :], src[...]).astype(BF16)
        tiles(n_dp, body)

    def views(l, which):
        if which == 2:
            return part_dn.at[l], land_dn, mid_dn, own_dn.at[l], lambda s: land_dn.at[s, l], lambda s: mid_dn.at[s, l], 1
        return (
            part_gu.at[l, which], land_gu, mid_gu, own_gu.at[l, which],
            lambda s: land_gu.at[s, l, which], lambda s: mid_gu.at[s, l, which], 0,
        )

    def reduce_begin(l, which):
        part, _, _, own, land, mid, kind = views(l, which)
        half = part.shape[1] // 2
        low, high = pl.ds(0, half), pl.ds(half, half)
        slot = 3 * l + which
        pltpu.make_async_copy(part.at[dp], own, own_sem.at[kind]).start()
        for to, side, mine, theirs in ((right, 0, low, high), (left, 1, high, low)):
            pltpu.make_async_remote_copy(
                src_ref=part.at[across, mine], dst_ref=mid(side),
                send_sem=rs_send.at[slot], recv_sem=mid_recv.at[slot],
                device_id={"dp": to}, device_id_type=MESH,
            ).start()
        for to, side, mine, theirs in ((right, 0, low, high), (left, 1, high, low)):
            pltpu.make_async_remote_copy(
                src_ref=part.at[to, theirs], dst_ref=land(side).at[theirs],
                send_sem=rs_send.at[slot], recv_sem=land_sem.at[kind],
                device_id={"dp": to}, device_id_type=MESH,
            ).start()

    def reduce_pass(l, which):
        part, _, mids, own, land, mid, kind = views(l, which)
        half = part.shape[1] // 2
        slot = 3 * l + which
        both = mid_dn.at[:, l] if which == 2 else mid_gu.at[:, l, which]
        pltpu.make_async_copy(both, both, mid_recv.at[slot]).wait()
        for to, side, start in ((right, 0, 0), (left, 1, half)):
            mine = pl.ds(start, half)
            step = half // 4

            def body(i):
                at = pl.ds(pl.multiple_of(start + i * step, step), step)
                part[to, at] = (
                    part[to, at].astype(F32) + mid(side)[span(i, step)].astype(F32)
                ).astype(BF16)

            tiles(4, body)
            pltpu.make_async_remote_copy(
                src_ref=part.at[to, mine], dst_ref=land(side).at[mine],
                send_sem=rs_send.at[slot], recv_sem=land_sem.at[kind],
                device_id={"dp": to}, device_id_type=MESH,
            ).start()

    def load_back(i):
        return pltpu.make_async_copy(back.at[i], recv.at[i], load_sem.at[i])

    def combine_out(l):
        i = 2 * l
        load_back(i).wait()
        prob = pslot[l]
        hit = sel[l].astype(F32)
        weight = (hit * prob).T
        hi = weight.astype(BF16)
        lo = (weight - hi.astype(F32)).astype(BF16)

        def body(n):
            cols = span(n, d_tile)
            value = dot(hi, recv[i, :, cols]) + dot(lo, recv[i, :, cols])
            if l == 0:
                acc[0, :, cols] = value
            else:
                lo_ref[:, cols] = (acc[0, :, cols] + value).astype(BF16)
        tiles(n_d, body)
        inner = dot(og_ref[...], recv[i], NT)
        inner = inner * sel_t[l].astype(F32)
        expert = lax.broadcasted_iota(jnp.int32, (tok, rows), 1) // CAP * 2 + l
        for k in range(top):
            hit = expert == ids_ref[:, k : k + 1]
            value = jnp.sum(jnp.where(hit, inner, 0.0), axis=1, keepdims=True)
            if l == 0:
                gg_ref[:, k : k + 1] = value
            else:
                gg_ref[:, k : k + 1] = gg_ref[:, k : k + 1] + value

    def combine_grad(l):
        i = 2 * l + 1
        load_back(i).wait()

        def body(n):
            cols = span(n, d_tile)
            value = dot(sel_t[l], recv[i, :, cols])
            if l == 0:
                acc[1, :, cols] = value
            else:
                tg_ref[:, cols] = (acc[1, :, cols] + value).astype(BF16)
        tiles(n_d, body)

    route(0)
    fill_tokens(0)
    pl.semaphore_wait(barrier, n_exp - 1 + 2)
    exchange(0, recv, disp_send, disp_recv)
    fill_delta(0)
    exchange(1, recv, disp_send, disp_recv)
    route(1)
    fill_tokens(1)
    fill_delta(1)

    for copy in weights(0):
        copy.wait()
    wait_landed(0, recv, disp_recv)
    wait_sent(0, disp_send)
    exchange(2, recv, disp_send, disp_recv)
    forward(0)
    turn_tokens(0)
    outputs(0)

    wait_landed(1, recv, disp_recv)
    wait_sent(1, disp_send)
    exchange(3, recv, disp_send, disp_recv)
    down_part(0)
    reduce_begin(0, 2)
    deltas(0)
    gate_up_part(0, 0)
    reduce_begin(0, 0)
    gate_up_part(0, 1)
    reduce_begin(0, 1)
    input_grads(0)
    for copy in weights(1):
        copy.start()

    wait_landed(2, recv, disp_recv)
    wait_sent(2, disp_send)
    for copy in weights(1):
        copy.wait()
    forward(1)
    turn_tokens(1)
    outputs(1)
    reduce_pass(0, 2)

    wait_landed(3, recv, disp_recv)
    wait_sent(3, disp_send)
    exchange(0, back, back_send, back_recv)
    exchange(1, back, back_send, back_recv)
    down_part(1)
    reduce_begin(1, 2)
    reduce_pass(0, 0)
    deltas(1)
    gate_up_part(1, 0)
    reduce_begin(1, 0)
    gate_up_part(1, 1)
    reduce_begin(1, 1)
    exchange(2, back, back_send, back_recv)
    input_grads(1)
    exchange(3, back, back_send, back_recv)
    reduce_pass(0, 1)

    for i in (0, 1):
        wait_landed(i, back, back_recv)
        load_back(i).start()
    combine_out(0)
    combine_grad(0)
    reduce_pass(1, 2)
    reduce_pass(1, 0)
    wait_landed(2, back, back_recv)
    load_back(2).start()
    combine_out(1)
    reduce_pass(1, 1)
    wait_landed(3, back, back_recv)
    load_back(3).start()
    combine_grad(1)

    for i in range(4):
        wait_sent(i, back_send)
    for which in range(3):
        for l in range(2):
            three = part_dn.at[l, pl.ds(0, 3)] if which == 2 else part_gu.at[l, which, pl.ds(0, 3)]
            pltpu.make_async_copy(three, three, rs_send.at[3 * l + which]).wait()
    pltpu.make_async_copy(own_gu, own_gu, own_sem.at[0]).wait()
    pltpu.make_async_copy(own_dn, own_dn, own_sem.at[1]).wait()
    pltpu.make_async_copy(land_gu, land_gu, land_sem.at[0]).wait()
    pltpu.make_async_copy(land_dn, land_dn, land_sem.at[1]).wait()


def shards(n_dp, n_exp, tokens, expert_ids, gate_probs, w_gate, w_up, w_down, out_grad):
    tok, feats = tokens.shape
    hidden = w_gate.shape[2]
    rows = n_exp * CAP
    share = feats // n_dp
    route = jnp.concatenate([expert_ids.astype(F32), gate_probs], axis=1).T
    vmem = pl.BlockSpec(memory_space=pltpu.VMEM)
    far = pl.BlockSpec(memory_space=pl.ANY)
    shape = jax.ShapeDtypeStruct
    top = expert_ids.shape[1]
    outs = pl.pallas_call(
        functools.partial(kernel, n_dp, n_exp),
        out_shape=[
            shape((tok, feats), BF16),
            shape((tok, feats), BF16),
            shape((tok, top), F32),
            shape((2, 2, share, hidden), BF16),
            shape((2, hidden, share), BF16),
            shape((2, 2, 2, share, hidden), BF16),
            shape((2, 2, hidden, share), BF16),
            shape((4, rows, feats), BF16),
        ],
        in_specs=[vmem] * 4 + [far] * 3,
        out_specs=[vmem] * 3 + [far] * 5,
        scratch_shapes=[
            pltpu.VMEM((4, rows, feats), BF16),
            pltpu.VMEM((4, rows, feats), BF16),
            pltpu.VMEM((feats, rows), BF16),
            pltpu.VMEM((feats, hidden), BF16),
            pltpu.VMEM((feats, hidden), BF16),
            pltpu.VMEM((hidden, feats), BF16),
            pltpu.VMEM((rows, hidden), BF16),
            pltpu.VMEM((hidden, rows), BF16),
            pltpu.VMEM((rows, hidden), BF16),
            pltpu.VMEM((rows, hidden), BF16),
            pltpu.VMEM((rows, hidden), F32),
            pltpu.VMEM((rows, hidden), F32),
            pltpu.VMEM((2, 2, n_dp, share, hidden), BF16),
            pltpu.VMEM((2, n_dp, hidden, share), BF16),
            pltpu.VMEM((2, 2, 2, share // 2, hidden), BF16),
            pltpu.VMEM((2, 2, hidden // 2, share), BF16),
            pltpu.VMEM((2, rows, tok), BF16),
            pltpu.VMEM((2, tok, rows), BF16),
            pltpu.VMEM((2, rows, 1), F32),
            pltpu.VMEM((2, tok, feats), F32),
            pltpu.SemaphoreType.DMA((3,)),
            pltpu.SemaphoreType.DMA((4,)),
            pltpu.SemaphoreType.DMA((4,)),
            pltpu.SemaphoreType.DMA((4,)),
            pltpu.SemaphoreType.DMA((4,)),
            pltpu.SemaphoreType.DMA((6,)),
            pltpu.SemaphoreType.DMA((6,)),
            pltpu.SemaphoreType.DMA((2,)),
            pltpu.SemaphoreType.DMA((2,)),
            pltpu.SemaphoreType.DMA((4,)),
        ],
        compiler_params=pltpu.CompilerParams(
            collective_id=0, has_side_effects=True, vmem_limit_bytes=62 * 2**20
        ),
        cost_estimate=pl.CostEstimate(
            flops=18 * 2 * rows * feats * hidden, bytes_accessed=60_000_000, transcendentals=4 * rows * hidden
        ),
    )(route, expert_ids, tokens, out_grad, w_gate, w_up, w_down)
    layer_out, token_grad, gate_grad, own_gu, own_dn, land_gu, land_dn, _ = outs
    wide = lambda a: a.astype(F32)
    total_gu = lambda i: wide(own_gu[:, i]) + wide(land_gu[0, :, i]) + wide(land_gu[1, :, i])
    grad_down = wide(own_dn) + wide(land_dn[0]) + wide(land_dn[1])
    return layer_out, token_grad, gate_grad, total_gu(0), total_gu(1), grad_down


def solution(mesh):
    tokens_at = P(("dp", "expert"), None)
    in_specs = (tokens_at,) * 3 + (P("expert", None, None),) * 3 + (tokens_at,)
    out_specs = (tokens_at,) * 3 + (
        P("expert", "dp", None),
        P("expert", "dp", None),
        P("expert", None, "dp"),
    )
    body = functools.partial(shards, mesh.shape["dp"], mesh.shape["expert"])
    return jax.shard_map(body, mesh=mesh, in_specs=in_specs, out_specs=out_specs, check_vma=False)
```

time: 373 us -> 236 us (0.63); the launches traced: 368 us -> 235 us
  Pallas kernels: 0 us -> 219 us
  waiting for transfers between devices: 145 us -> 0 us
  matrix products: 76.4 us -> 0 us
  local copies, waits for them, and re-layouts: 72.2 us -> 4.5 us
  starting transfers between devices: 34.5 us -> 0 us
  other arithmetic: 25.3 us -> 11.5 us
  between operations: 14.3 us -> 0.65 us
    pallas_call x0 -> x1, Pallas kernels: none -> 219 us  [shards(): pl.pallas_call(functools.partial(kernel, n_dp, n_exp), out_shape=[shape((...]
    all_to_all x4 -> x0, waiting for transfers between devices: 125 us -> none  [the longest x1 32.5 us: shards(): lax.all_to_all(send_delta, 'expert', split_axis=1, concat_axis=1, tiled=T...]
    dot_general x10 -> x0, matrix products: 76.4 us -> none  [the longest x1 10.1 us: shards(): jnp.einsum('esf,edf->esd', gate_delta, w_gate, preferred_element_type=jnp...]
    all_to_all x4 -> x0, starting transfers between devices: 33.6 us -> none  [the longest x1 9.79 us: shards(): lax.all_to_all(send_tokens, 'expert', split_axis=1, concat_axis=1, tiled=...]
    gather x5 -> x0, local copies, waits for them, and re-layouts: 33.3 us -> none  [the longest x1 7.26 us: shards(): back_rows.reshape(slot_count, features)[slot_index]]
    reduce_scatter x3 -> x0, waiting for transfers between devices: 19.7 us -> none  [the longest x1 19.7 us: shards(): lax.psum_scatter(gate_part.astype(jnp.bfloat16), 'dp', scatter_dimension=...]
    all_to_all x4 -> x0, local copies, waits for them, and re-layouts: 14.8 us -> none  [the longest x1 4.75 us: shards(): lax.all_to_all(expert_out.reshape(local_count, owners, capacity, features...]
    reshape x7 -> x0, local copies, waits for them, and re-layouts: 14.4 us -> none  [the longest x1 4.74 us: shards(): jnp.concatenate([tokens, zero_row], axis=0)[tok_index]]
  transfers between devices with their start and end apart: 7 -> 0, of which waited for: 5 -> 0; matrix products, arithmetic and copies ran while one was open for 37% -> 0% of each run, Pallas kernels for 0% -> 0%
where the time goes in v1:
time: 236 us; the launch traced here: 235 us
  Pallas kernels  219 us (93%)
  other arithmetic  11.5 us (5%)
  local copies, waits for them, and re-layouts  4.5 us (2%)
    pallas_call x1, Pallas kernels, shards(): pl.pallas_call(functools.partial(kernel, n_dp, n_exp), out_shape=[shape((...  219 us
    add x1, other arithmetic, shards(): grad_down = wide(own_dn) + wide(land_dn[0]) + wide(land_dn[1])  4.85 us

profile of v1, /device:TPU:1, one launch (start us, length us, event | category | flops | bytes accessed | tf_op | source)
XLA Modules:
  0.0 235.3 jit_solution(8740987356453527110)
XLA Ops:
  0.6 0.7 convert_element_type.54
  1.3 1.3 maximum_bitcast_fusion.route_ref
  2.6 1.4 copy.13.ids_ref
  4.0 218.7 %shard_map.118 = (bf16[128,2048]{1,0:T(8,128)(2,1)}, bf16[128,2048]{1,0:T(8,128)(2,1)}, f32[128,4]{1,0:T(8,128)}, bf16[2,2,512,768]{3,2,1,0:T(8,128)(2,1)}, bf16...) custom-call(f32[8,128]{1,0:T(8,128)} %maximum_bitcast_fusion.route_r, ...), custom_call_target="tpu_custom_call" | custom-call | flops 28991029248 | bytes 60000000 | tf_op jit(solution)/shard_map/pallas_call | solution.py:389
  222.7 1.5 copy.18
  224.2 0.0 copy-start
  224.2 4.8 %convert_add_fusion = f32[2,768,512]{2,1,0:T(8,128)} fusion(bf16[2,768,512]{2,1,0:T(8,128)(2,1)} %get-tuple-element.18, bf16[2,2,768,512]{3,2,1,0:T(8,128)(2,1)} %get-tuple-element.19), kind=kLoop, calls=%fused_computation | loop fusion | flops 3932160 | bytes 7864320 | tf_op jit(solution)/shard_map/add | solution.py:445
  229.1 0.0 copy-done
  229.1 0.0 copy-start.2
  229.1 0.0 copy-start.1
  229.1 4.7 %convert_add_fusion.2 = (f32[2,512,768]{2,1,0:T(8,128)}, f32[2,512,768]{2,1,0:T(8,128)}) fusion(bf16[2,2,2,512,768]{4,3,2,1,0:T(8,128)(2,1)S(1)} %copy-done, bf16[2,2,512,768]{3,2,1,0:T(8,128)(2,1)} %get-tuple-element.16), kind=kLoop, calls=%fused_computation.2 | loop fusion | flops 7864320 | bytes 15728640 | tf_op jit(solution)/shard_map/add | solution.py:444
  233.7 0.0 copy-done.2
  233.7 0.8 copy.25
  234.5 0.0 copy-done.1
  234.5 0.8 copy.26
Async XLA Ops:
  224.2 4.9 %copy-start = (bf16[2,2,2,512,768]{4,3,2,1,0:T(8,128)(2,1)S(1)}, bf16[2,2,2,512,768]{4,3,2,1,0:T(8,128)(2,1)}, u32[]{:S(2)}) copy-start(bf16[2,2,2,512,768]{4,3,2,1,0:T(8,128)(2,1)} %get-tuple-element.17) | copy-start | bytes 18874372
  229.1 4.7 %copy-start.2 = (bf16[128,2048]{1,0:T(8,128)(2,1)S(1)}, bf16[128,2048]{1,0:T(8,128)(2,1)}, u32[]{:S(2)}) copy-start(bf16[128,2048]{1,0:T(8,128)(2,1)} %get-tuple-element.34) | copy-start | bytes 1572868
  229.1 5.5 %copy-start.1 = (bf16[128,2048]{1,0:T(8,128)(2,1)S(1)}, bf16[128,2048]{1,0:T(8,128)(2,1)}, u32[]{:S(2)}) copy-start(bf16[128,2048]{1,0:T(8,128)(2,1)} %get-tuple-element.35) | copy-start | bytes 1572868

commit v2 on v1

--- a/solution.py
+++ b/solution.py
@@ -32,18 +32,18 @@
 
 def kernel(
     n_dp, n_exp,
-    route_ref, ids_ref, tok_ref, og_ref, wg_hbm, wu_hbm, wd_hbm,
-    lo_ref, tg_ref, gg_ref, own_gu, own_dn, land_gu, land_dn, back,
+    ids_ref, probs_ref, tok_ref, og_ref, wg_hbm, wu_hbm, wd_hbm,
+    lo_ref, tg_ref, gg_ref, sum_gu, sum_dn, land_gu, land_dn, back,
     send, recv, tt, wg, wu, wd, act, act_t, gd, ud, pre_g, pre_u,
     part_gu, part_dn, mid_gu, mid_dn, sel, sel_t, pslot, acc,
-    w_sem, disp_send, disp_recv, back_send, back_recv,
-    rs_send, mid_recv, land_sem, own_sem, load_sem,
+    w_sem, disp_send, tok_recv, delta_recv, back_send, back_recv,
+    rs_send, mid_recv, land_recv, sum_sem, load_sem,
 ):
     dp, me = lax.axis_index("dp"), lax.axis_index("expert")
     tok, feats = tok_ref.shape
     hidden = wg.shape[1]
     rows = n_exp * CAP
-    top = ids_ref.shape[1]
+    top = ids_ref.shape[0]
     right, left = lax.rem(dp + 1, n_dp), lax.rem(dp + n_dp - 1, n_dp)
     across = lax.rem(dp + 2, n_dp)
     f_tile, d_tile = min(256, hidden), min(256, feats)
@@ -79,14 +79,14 @@
     for copy in weights(0):
         copy.start()
 
-    ids_t, probs_t = route_ref[0:top, :], route_ref[top : 2 * top, :]
+    ids_t, probs_t = ids_ref[...], probs_ref[...]
     earlier = (
         lax.broadcasted_iota(jnp.int32, (tok, tok), 0)
         < lax.broadcasted_iota(jnp.int32, (tok, tok), 1)
     ).astype(F32).astype(BF16)
 
     def route(l):
-        expert = (lax.broadcasted_iota(jnp.int32, (n_exp, tok), 0) * 2 + l).astype(F32)
+        expert = lax.broadcasted_iota(jnp.int32, (n_exp, tok), 0) * 2 + l
         named = jnp.zeros((n_exp, tok), F32)
         prob = jnp.zeros((n_exp, tok), F32)
         for k in range(top):
@@ -118,16 +118,20 @@
     def chunk(i):
         return pl.ds(pl.multiple_of(i * CAP, CAP), CAP)
 
-    def exchange(i, land, send_sem, recv_sem):
-        pltpu.make_async_copy(send.at[i, chunk(me)], land.at[i, chunk(me)], recv_sem.at[i]).start()
+    everything = pl.ds(0, feats)
+
+    def exchange(i, land, cols, send_sem, recv_sem):
+        pltpu.make_async_copy(
+            send.at[i, chunk(me), cols], land.at[i, chunk(me), cols], recv_sem
+        ).start()
 
         def body(k, carry):
             to = peer(k)
             pltpu.make_async_remote_copy(
-                src_ref=send.at[i, chunk(to)],
-                dst_ref=land.at[i, chunk(me)],
-                send_sem=send_sem.at[i],
-                recv_sem=recv_sem.at[i],
+                src_ref=send.at[i, chunk(to), cols],
+                dst_ref=land.at[i, chunk(me), cols],
+                send_sem=send_sem,
+                recv_sem=recv_sem,
                 device_id={"expert": to},
                 device_id_type=MESH,
             ).start()
@@ -139,8 +143,26 @@
         part = send.at[i, pl.ds(0, rows - CAP)]
         pltpu.make_async_copy(part, part, sem.at[i]).wait()
 
-    def wait_landed(i, land, sem):
-        pltpu.make_async_copy(land.at[i], land.at[i], sem.at[i]).wait()
+    def wait_landed(view, sem):
+        pltpu.make_async_copy(view, view, sem).wait()
+
+    order = (across, right, left, dp)
+
+    def send_tokens(l):
+        exchange(2 * l, recv, everything, disp_send.at[2 * l], tok_recv.at[l])
+
+    def send_delta(l):
+        for n, j in enumerate(order):
+            exchange(2 * l + 1, recv, span(j, share), disp_send.at[2 * l + 1], delta_recv.at[l, n])
+
+    def tokens_landed(l):
+        wait_landed(recv.at[2 * l], tok_recv.at[l])
+
+    def delta_landed(l, n):
+        wait_landed(recv.at[2 * l + 1, :, span(order[n], share)], delta_recv.at[l, n])
+
+    def send_back(i):
+        exchange(i, back, everything, back_send.at[i], back_recv.at[i])
 
     def forward(l):
         def body(i):
@@ -184,53 +206,62 @@
             ).astype(BF16)
         tiles(n_d, body)
 
+    def views(l, which):
+        if which == 2:
+            return part_dn.at[l], lambda s: land_dn.at[s, l], lambda s: mid_dn.at[s, l]
+        return part_gu.at[l, which], lambda s: land_gu.at[s, l, which], lambda s: mid_gu.at[s, l, which]
+
+    def post(l, which, src, dst, sem, to):
+        pltpu.make_async_remote_copy(
+            src_ref=src, dst_ref=dst, send_sem=rs_send.at[3 * l + which], recv_sem=sem.at[3 * l + which],
+            device_id={"dp": to}, device_id_type=MESH,
+        ).start()
+
+    def reduce_begin(l, which, make, ready=None):
+        part, land, mid = views(l, which)
+        half = part.shape[1] // 2
+        low, high = pl.ds(0, half), pl.ds(half, half)
+        for n, j in enumerate(order):
+            if ready is not None:
+                ready(n)
+            make(j)
+            if n == 0:
+                post(l, which, part.at[j, low], mid(0), mid_recv, right)
+                post(l, which, part.at[j, high], mid(1), mid_recv, left)
+            elif n == 1:
+                post(l, which, part.at[j, high], land(0).at[high], land_recv, right)
+            elif n == 2:
+                post(l, which, part.at[j, low], land(1).at[low], land_recv, left)
+
     def down_part(l):
-        def body(j):
-            part_dn[l, j] = dot(act_t[...], recv[2 * l + 1, :, span(j, share)]).astype(BF16)
-        tiles(n_dp, body)
+        def make(j):
+            def body(i):
+                at = span(i, f_tile)
+                part_dn[l, j, at] = dot(act_t[at, :], recv[2 * l + 1, :, span(j, share)]).astype(BF16)
+
+            tiles(n_f, body)
+
+        reduce_begin(l, 2, make, lambda n: delta_landed(l, n))
 
     def gate_up_part(l, which):
         src = (gd, ud)[which]
 
-        def body(j):
-            part_gu[l, which, j] = dot(tt[span(j, share), :], src[...]).astype(BF16)
-        tiles(n_dp, body)
-
-    def views(l, which):
-        if which == 2:
-            return part_dn.at[l], land_dn, mid_dn, own_dn.at[l], lambda s: land_dn.at[s, l], lambda s: mid_dn.at[s, l], 1
-        return (
-            part_gu.at[l, which], land_gu, mid_gu, own_gu.at[l, which],
-            lambda s: land_gu.at[s, l, which], lambda s: mid_gu.at[s, l, which], 0,
-        )
-
-    def reduce_begin(l, which):
-        part, _, _, own, land, mid, kind = views(l, which)
+        def make(j):
+            def body(i):
+                at = span(i, d_tile)
+                turned = tt[pl.ds(pl.multiple_of(j * share + i * d_tile, d_tile), d_tile), :]
+                part_gu[l, which, j, at] = dot(turned, src[...]).astype(BF16)
+
+            tiles(share // d_tile, body)
+
+        reduce_begin(l, which, make)
+
+    def reduce_pass(l, which):
+        part, land, mid = views(l, which)
         half = part.shape[1] // 2
-        low, high = pl.ds(0, half), pl.ds(half, half)
-        slot = 3 * l + which
-        pltpu.make_async_copy(part.at[dp], own, own_sem.at[kind]).start()
-        for to, side, mine, theirs in ((right, 0, low, high), (left, 1, high, low)):
-            pltpu.make_async_remote_copy(
-                src_ref=part.at[across, mine], dst_ref=mid(side),
-                send_sem=rs_send.at[slot], recv_sem=mid_recv.at[slot],
-                device_id={"dp": to}, device_id_type=MESH,
-            ).start()
-        for to, side, mine, theirs in ((right, 0, low, high), (left, 1, high, low)):
-            pltpu.make_async_remote_copy(
-                src_ref=part.at[to, theirs], dst_ref=land(side).at[theirs],
-                send_sem=rs_send.at[slot], recv_sem=land_sem.at[kind],
-                device_id={"dp": to}, device_id_type=MESH,
-            ).start()
-
-    def reduce_pass(l, which):
-        part, _, mids, own, land, mid, kind = views(l, which)
-        half = part.shape[1] // 2
-        slot = 3 * l + which
         both = mid_dn.at[:, l] if which == 2 else mid_gu.at[:, l, which]
-        pltpu.make_async_copy(both, both, mid_recv.at[slot]).wait()
+        wait_landed(both, mid_recv.at[3 * l + which])
         for to, side, start in ((right, 0, 0), (left, 1, half)):
-            mine = pl.ds(start, half)
             step = half // 4
 
             def body(i):
@@ -240,11 +271,45 @@
                 ).astype(BF16)
 
             tiles(4, body)
-            pltpu.make_async_remote_copy(
-                src_ref=part.at[to, mine], dst_ref=land(side).at[mine],
-                send_sem=rs_send.at[slot], recv_sem=land_sem.at[kind],
-                device_id={"dp": to}, device_id_type=MESH,
-            ).start()
+            mine = pl.ds(start, half)
+            post(l, which, part.at[to, mine], land(side).at[mine], land_recv, to)
+
+    def landing(l, which, side):
+        if which == 2:
+            return land_dn.at[side, l], wd.at[:, pl.ds((2 * l + side) * share, share)]
+        return land_gu.at[side, l, which], (wg, wu)[which].at[pl.ds((2 * l + side) * share, share)]
+
+    def fetch(l, which):
+        return [
+            pltpu.make_async_copy(*landing(l, which, side), sum_sem.at[3 * l + which, side])
+            for side in range(2)
+        ]
+
+    def reduce_fetch(l, which):
+        both = land_dn.at[:, l] if which == 2 else land_gu.at[:, l, which]
+        wait_landed(both, land_recv.at[3 * l + which])
+        for copy in fetch(l, which):
+            copy.start()
+
+    def total_out(l, which):
+        src, dst = (part_dn.at[l], sum_dn.at[l]) if which == 2 else (part_gu.at[l, which], sum_gu.at[which, l])
+        return pltpu.make_async_copy(src.at[dp], dst, sum_sem.at[3 * l + which, 2])
+
+    def reduce_end(l, which):
+        for copy in fetch(l, which):
+            copy.wait()
+        part = views(l, which)[0]
+        first, second = (landing(l, which, side)[1] for side in range(2))
+        step = part.shape[1] // 4
+
+        def body(i):
+            at = span(i, step)
+            part[dp, at] = (
+                part[dp, at].astype(F32) + first[at].astype(F32) + second[at].astype(F32)
+            ).astype(BF16)
+
+        tiles(4, body)
+        total_out(l, which).start()
 
     def load_back(i):
         return pltpu.make_async_copy(back.at[i], recv.at[i], load_sem.at[i])
@@ -266,16 +331,16 @@
             else:
                 lo_ref[:, cols] = (acc[0, :, cols] + value).astype(BF16)
         tiles(n_d, body)
-        inner = dot(og_ref[...], recv[i], NT)
-        inner = inner * sel_t[l].astype(F32)
-        expert = lax.broadcasted_iota(jnp.int32, (tok, rows), 1) // CAP * 2 + l
+        inner = dot(recv[i], og_ref[...], NT) * hit
+        inner = jnp.sum(inner.reshape(n_exp, CAP, tok), axis=1)
+        expert = lax.broadcasted_iota(jnp.int32, (n_exp, tok), 0) * 2 + l
         for k in range(top):
-            hit = expert == ids_ref[:, k : k + 1]
-            value = jnp.sum(jnp.where(hit, inner, 0.0), axis=1, keepdims=True)
+            mine = jnp.where(expert == ids_t[k : k + 1, :], inner, 0.0)
+            value = jnp.sum(mine, axis=0, keepdims=True)
             if l == 0:
-                gg_ref[:, k : k + 1] = value
+                gg_ref[k : k + 1, :] = value
             else:
-                gg_ref[:, k : k + 1] = gg_ref[:, k : k + 1] + value
+                gg_ref[k : k + 1, :] = gg_ref[k : k + 1, :] + value
 
     def combine_grad(l):
         i = 2 * l + 1
@@ -293,87 +358,86 @@
     route(0)
     fill_tokens(0)
     pl.semaphore_wait(barrier, n_exp - 1 + 2)
-    exchange(0, recv, disp_send, disp_recv)
+    send_tokens(0)
     fill_delta(0)
-    exchange(1, recv, disp_send, disp_recv)
+    send_delta(0)
     route(1)
     fill_tokens(1)
+    send_tokens(1)
     fill_delta(1)
+    send_delta(1)
 
     for copy in weights(0):
         copy.wait()
-    wait_landed(0, recv, disp_recv)
-    wait_sent(0, disp_send)
-    exchange(2, recv, disp_send, disp_recv)
+    tokens_landed(0)
     forward(0)
+    down_part(0)
     turn_tokens(0)
-    outputs(0)
-
-    wait_landed(1, recv, disp_recv)
-    wait_sent(1, disp_send)
-    exchange(3, recv, disp_send, disp_recv)
-    down_part(0)
-    reduce_begin(0, 2)
+    reduce_pass(0, 2)
     deltas(0)
     gate_up_part(0, 0)
-    reduce_begin(0, 0)
     gate_up_part(0, 1)
-    reduce_begin(0, 1)
+    wait_sent(0, disp_send)
+    outputs(0)
+    send_back(0)
+    wait_sent(1, disp_send)
     input_grads(0)
+    send_back(1)
     for copy in weights(1):
         copy.start()
 
-    wait_landed(2, recv, disp_recv)
-    wait_sent(2, disp_send)
+    tokens_landed(1)
     for copy in weights(1):
         copy.wait()
     forward(1)
     turn_tokens(1)
+    reduce_pass(0, 0)
+    wait_sent(2, disp_send)
     outputs(1)
-    reduce_pass(0, 2)
-
-    wait_landed(3, recv, disp_recv)
-    wait_sent(3, disp_send)
-    exchange(0, back, back_send, back_recv)
-    exchange(1, back, back_send, back_recv)
+    send_back(2)
+    reduce_pass(0, 1)
     down_part(1)
-    reduce_begin(1, 2)
-    reduce_pass(0, 0)
     deltas(1)
     gate_up_part(1, 0)
-    reduce_begin(1, 0)
     gate_up_part(1, 1)
-    reduce_begin(1, 1)
-    exchange(2, back, back_send, back_recv)
+    wait_sent(3, disp_send)
     input_grads(1)
-    exchange(3, back, back_send, back_recv)
-    reduce_pass(0, 1)
-
-    for i in (0, 1):
-        wait_landed(i, back, back_recv)
-        load_back(i).start()
+    send_back(3)
+
+    reduce_fetch(0, 2)
+    reduce_end(0, 2)
+    reduce_fetch(0, 0)
+    reduce_fetch(0, 1)
+    wait_landed(back.at[0], back_recv.at[0])
+    load_back(0).start()
+    reduce_end(0, 0)
+    reduce_end(0, 1)
     combine_out(0)
+    reduce_pass(1, 2)
+    wait_landed(back.at[1], back_recv.at[1])
+    load_back(1).start()
     combine_grad(0)
-    reduce_pass(1, 2)
     reduce_pass(1, 0)
-    wait_landed(2, back, back_recv)
+    reduce_pass(1, 1)
+    wait_landed(back.at[2], back_recv.at[2])
     load_back(2).start()
     combine_out(1)
-    reduce_pass(1, 1)
-    wait_landed(3, back, back_recv)
+    for which in (2, 0):
+        reduce_fetch(1, which)
+        reduce_end(1, which)
+    wait_landed(back.at[3], back_recv.at[3])
     load_back(3).start()
+    reduce_fetch(1, 1)
     combine_grad(1)
+    reduce_end(1, 1)
 
     for i in range(4):
         wait_sent(i, back_send)
-    for which in range(3):
-        for l in range(2):
+    for l in range(2):
+        for which in range(3):
             three = part_dn.at[l, pl.ds(0, 3)] if which == 2 else part_gu.at[l, which, pl.ds(0, 3)]
-            pltpu.make_async_copy(three, three, rs_send.at[3 * l + which]).wait()
-    pltpu.make_async_copy(own_gu, own_gu, own_sem.at[0]).wait()
-    pltpu.make_async_copy(own_dn, own_dn, own_sem.at[1]).wait()
-    pltpu.make_async_copy(land_gu, land_gu, land_sem.at[0]).wait()
-    pltpu.make_async_copy(land_dn, land_dn, land_sem.at[1]).wait()
+            wait_landed(three, rs_send.at[3 * l + which])
+            total_out(l, which).wait()
 
 
 def shards(n_dp, n_exp, tokens, expert_ids, gate_probs, w_gate, w_up, w_down, out_grad):
@@ -381,7 +445,6 @@
     hidden = w_gate.shape[2]
     rows = n_exp * CAP
     share = feats // n_dp
-    route = jnp.concatenate([expert_ids.astype(F32), gate_probs], axis=1).T
     vmem = pl.BlockSpec(memory_space=pltpu.VMEM)
     far = pl.BlockSpec(memory_space=pl.ANY)
     shape = jax.ShapeDtypeStruct
@@ -391,7 +454,7 @@
         out_shape=[
             shape((tok, feats), BF16),
             shape((tok, feats), BF16),
-            shape((tok, top), F32),
+            shape((top, tok), F32),
             shape((2, 2, share, hidden), BF16),
             shape((2, hidden, share), BF16),
             shape((2, 2, 2, share, hidden), BF16),
@@ -423,13 +486,14 @@
             pltpu.VMEM((2, tok, feats), F32),
             pltpu.SemaphoreType.DMA((3,)),
             pltpu.SemaphoreType.DMA((4,)),
-            pltpu.SemaphoreType.DMA((4,)),
+            pltpu.SemaphoreType.DMA((2,)),
+            pltpu.SemaphoreType.DMA((2, 4)),
             pltpu.SemaphoreType.DMA((4,)),
             pltpu.SemaphoreType.DMA((4,)),
             pltpu.SemaphoreType.DMA((6,)),
             pltpu.SemaphoreType.DMA((6,)),
-            pltpu.SemaphoreType.DMA((2,)),
-            pltpu.SemaphoreType.DMA((2,)),
+            pltpu.SemaphoreType.DMA((6,)),
+            pltpu.SemaphoreType.DMA((6, 3)),
             pltpu.SemaphoreType.DMA((4,)),
         ],
         compiler_params=pltpu.CompilerParams(
@@ -438,12 +502,9 @@
         cost_estimate=pl.CostEstimate(
             flops=18 * 2 * rows * feats * hidden, bytes_accessed=60_000_000, transcendentals=4 * rows * hidden
         ),
-    )(route, expert_ids, tokens, out_grad, w_gate, w_up, w_down)
-    layer_out, token_grad, gate_grad, own_gu, own_dn, land_gu, land_dn, _ = outs
-    wide = lambda a: a.astype(F32)
-    total_gu = lambda i: wide(own_gu[:, i]) + wide(land_gu[0, :, i]) + wide(land_gu[1, :, i])
-    grad_down = wide(own_dn) + wide(land_dn[0]) + wide(land_dn[1])
-    return layer_out, token_grad, gate_grad, total_gu(0), total_gu(1), grad_down
+    )(expert_ids.T, gate_probs.T, tokens, out_grad, w_gate, w_up, w_down)
+    layer_out, token_grad, gate_grad, sum_gu, sum_dn, *_ = outs
+    return layer_out, token_grad, gate_grad.T, sum_gu[0].astype(F32), sum_gu[1].astype(F32), sum_dn.astype(F32)
 
 
 def solution(mesh):

time: 236 us -> 214 us (0.907)
  Pallas kernels: 219 us -> 204 us
  other arithmetic: 11.5 us -> 6.91 us
    pallas_call x1, Pallas kernels: 219 us -> 204 us  [shards(): pl.pallas_call(functools.partial(kernel, n_dp, n_exp), out_shape=[shape((...]
    add x2 -> x0, other arithmetic: 9.52 us -> none  [the longest x1 4.85 us: shards(): grad_down = wide(own_dn) + wide(land_dn[0]) + wide(land_dn[1])]
    convert_element_type x1 -> x2, other arithmetic: 0.69 us -> 6.91 us  [the longest x1 3.67 us: shards(): sum_dn.astype(F32)]
where the time goes in v2:
time: 214 us
  Pallas kernels  204 us (95%)
  other arithmetic  6.91 us (3%)
  local copies, waits for them, and re-layouts  2.18 us (1%)
    pallas_call x1, Pallas kernels, shards(): pl.pallas_call(functools.partial(kernel, n_dp, n_exp), out_shape=[shape((...  204 us

profile of v2, /device:TPU:1, one launch (start us, length us, event | category | flops | bytes accessed | tf_op | source)
XLA Modules:
  0.0 213.5 jit_solution(13964992107478105671)
XLA Ops:
  0.6 203.8 %shard_map.118 = (bf16[128,2048]{1,0:T(8,128)(2,1)}, bf16[128,2048]{1,0:T(8,128)(2,1)}, f32[4,128]{1,0:T(4,128)}, bf16[2,2,512,768]{3,2,1,0:T(8,128)(2,1)}, bf16...) custom-call(s32[4,128]{1,0:T(4,128)} %bitcast.10, ...), custom_call_target="tpu_custom_call" | custom-call | flops 28991029248 | bytes 60000000 | tf_op jit(solution)/shard_map/pallas_call | solution.py:452
  204.4 0.0 copy-start
  204.4 3.7 %convert_element_type.19 = f32[2,768,512]{2,1,0:T(8,128)} convert(bf16[2,768,512]{2,1,0:T(8,128)(2,1)} %get-tuple-element.15) | non-fusion elementwise | flops 786432 | bytes 4718592 | tf_op jit(solution)/shard_map/convert_element_type | solution.py:507
  208.1 0.0 copy-done
  208.1 0.0 copy-start.2
  208.1 0.0 copy-start.1
  208.1 0.0 copy-start.3
  208.1 3.2 %bitcast_convert_fusion = (f32[2,512,768]{2,1,0:T(8,128)}, f32[2,512,768]{2,1,0:T(8,128)}) fusion(bf16[2,2,512,768]{3,2,1,0:T(8,128)(2,1)S(1)} %copy-done), kind=kLoop, calls=%fused_computation | loop fusion | flops 1572864 | bytes 9437184 | tf_op jit(solution)/shard_map/convert_element_type | solution.py:507
  211.3 0.0 copy-done.2
  211.3 0.8 copy.16
  212.1 0.0 copy-done.1
  212.1 0.8 copy.17
  212.9 0.0 copy-done.3
  212.9 0.6 copy.18
Async XLA Ops:
  204.4 3.7 %copy-start = (bf16[2,2,512,768]{3,2,1,0:T(8,128)(2,1)S(1)}, bf16[2,2,512,768]{3,2,1,0:T(8,128)(2,1)}, u32[]{:S(2)}) copy-start(bf16[2,2,512,768]{3,2,1,0:T(8,128)(2,1)} %get-tuple-element.14) | copy-start | bytes 9437188
  208.1 3.3 %copy-start.2 = (bf16[128,2048]{1,0:T(8,128)(2,1)S(1)}, bf16[128,2048]{1,0:T(8,128)(2,1)}, u32[]{:S(2)}) copy-start(bf16[128,2048]{1,0:T(8,128)(2,1)} %get-tuple-element.24) | copy-start | bytes 1572868
  208.1 4.0 %copy-start.1 = (bf16[128,2048]{1,0:T(8,128)(2,1)S(1)}, bf16[128,2048]{1,0:T(8,128)(2,1)}, u32[]{:S(2)}) copy-start(bf16[128,2048]{1,0:T(8,128)(2,1)} %get-tuple-element.25) | copy-start | bytes 1572868
  208.1 4.8 %copy-start.3 = (f32[4,128]{1,0:T(4,128)S(1)}, f32[4,128]{1,0:T(4,128)}, u32[]{:S(2)}) copy-start(f32[4,128]{1,0:T(4,128)} %get-tuple-element.13) | copy-start | bytes 6148

commit v3 on v2

--- a/solution.py
+++ b/solution.py
@@ -35,8 +35,8 @@
     ids_ref, probs_ref, tok_ref, og_ref, wg_hbm, wu_hbm, wd_hbm,
     lo_ref, tg_ref, gg_ref, sum_gu, sum_dn, land_gu, land_dn, back,
     send, recv, tt, wg, wu, wd, act, act_t, gd, ud, pre_g, pre_u,
-    part_gu, part_dn, mid_gu, mid_dn, sel, sel_t, pslot, acc,
-    w_sem, disp_send, tok_recv, delta_recv, back_send, back_recv,
+    part_gu, part_dn, mid_gu, mid_dn, sel, pslot, acc,
+    w_sem, disp_send, tok_recv, delta_recv, back_send, back_recv, last_recv,
     rs_send, mid_recv, land_recv, sum_sem, load_sem,
 ):
     dp, me = lax.axis_index("dp"), lax.axis_index("expert")
@@ -100,14 +100,13 @@
         weight = jnp.sum(hit * prob[:, None, :], axis=2, keepdims=True)
         hit = hit.reshape(rows, tok)
         sel[l] = hit.astype(BF16)
-        sel_t[l] = hit.T.astype(BF16)
         pslot[l] = weight.reshape(rows, 1)
 
-    def fill_tokens(l):
-        def body(i):
-            cols = span(i, d_tile)
+    def fill_tokens(l, h):
+        def body(i):
+            cols = span(i + h * (n_d // 2), d_tile)
             send[2 * l, :, cols] = dot(sel[l], tok_ref[:, cols]).astype(BF16)
-        tiles(n_d, body)
+        tiles(n_d // 2, body)
 
     def fill_delta(l):
         def body(i):
@@ -146,20 +145,29 @@
     def wait_landed(view, sem):
         pltpu.make_async_copy(view, view, sem).wait()
 
-    order = (across, right, left, dp)
-
-    def send_tokens(l):
-        exchange(2 * l, recv, everything, disp_send.at[2 * l], tok_recv.at[l])
+    half_share = share // 2
+    pieces = tuple(
+        (j, h * half_share, half_share)
+        for j, h in ((across, 0), (across, 1), (right, 1), (left, 0), (right, 0), (left, 1))
+    ) + ((dp, 0, share),)
+    own = len(pieces) - 1
+
+    def piece(n):
+        j, start, size = pieces[n]
+        return pl.ds(pl.multiple_of(j * share + start, half_share), size)
+
+    def send_tokens(l, cols):
+        exchange(2 * l, recv, cols, disp_send.at[2 * l], tok_recv.at[l])
 
     def send_delta(l):
-        for n, j in enumerate(order):
-            exchange(2 * l + 1, recv, span(j, share), disp_send.at[2 * l + 1], delta_recv.at[l, n])
+        for n in range(len(pieces)):
+            exchange(2 * l + 1, recv, piece(n), disp_send.at[2 * l + 1], delta_recv.at[l, n])
 
     def tokens_landed(l):
         wait_landed(recv.at[2 * l], tok_recv.at[l])
 
     def delta_landed(l, n):
-        wait_landed(recv.at[2 * l + 1, :, span(order[n], share)], delta_recv.at[l, n])
+        wait_landed(recv.at[2 * l + 1, :, piece(n)], delta_recv.at[l, n])
 
     def send_back(i):
         exchange(i, back, everything, back_send.at[i], back_recv.at[i])
@@ -217,62 +225,73 @@
             device_id={"dp": to}, device_id_type=MESH,
         ).start()
 
-    def reduce_begin(l, which, make, ready=None):
-        part, land, mid = views(l, which)
-        half = part.shape[1] // 2
-        low, high = pl.ds(0, half), pl.ds(half, half)
-        for n, j in enumerate(order):
-            if ready is not None:
-                ready(n)
-            make(j)
-            if n == 0:
-                post(l, which, part.at[j, low], mid(0), mid_recv, right)
-                post(l, which, part.at[j, high], mid(1), mid_recv, left)
-            elif n == 1:
-                post(l, which, part.at[j, high], land(0).at[high], land_recv, right)
-            elif n == 2:
-                post(l, which, part.at[j, low], land(1).at[low], land_recv, left)
-
-    def down_part(l):
-        def make(j):
-            def body(i):
-                at = span(i, f_tile)
-                part_dn[l, j, at] = dot(act_t[at, :], recv[2 * l + 1, :, span(j, share)]).astype(BF16)
-
-            tiles(n_f, body)
-
-        reduce_begin(l, 2, make, lambda n: delta_landed(l, n))
+    def half(ref, which, h):
+        at = pl.ds(h * half_share, half_share)
+        return ref.at[:, at] if which == 2 else ref.at[at]
+
+    def post_across(l, which, h):
+        part, _, mid = views(l, which)
+        post(l, which, half(part.at[across], which, h), mid(h), mid_recv, (right, left)[h])
+
+    def post_direct(l, which, side):
+        part, land, _ = views(l, which)
+        to = (right, left)[side]
+        post(l, which, half(part.at[to], which, 1 - side), half(land(side), which, 1 - side), land_recv, to)
+
+    def make_down(l, n):
+        j, start, size = pieces[n]
+
+        def body(i):
+            at = span(i, f_tile)
+            part_dn[l, j, at, pl.ds(start, size)] = dot(act_t[at, :], recv[2 * l + 1, :, piece(n)]).astype(BF16)
+
+        tiles(n_f, body)
+
+    def down_part(l, meanwhile, later):
+        for h in range(2):
+            delta_landed(l, h)
+            make_down(l, h)
+            post_across(l, 2, h)
+        for side in range(2):
+            delta_landed(l, 2 + side)
+            make_down(l, 2 + side)
+            post_direct(l, 2, side)
+        meanwhile()
+        for n in (4, 5):
+            delta_landed(l, n)
+            make_down(l, n)
+        later()
+        delta_landed(l, own)
 
     def gate_up_part(l, which):
         src = (gd, ud)[which]
-
-        def make(j):
+        for n, j in enumerate((across, right, left, dp)):
+
             def body(i):
                 at = span(i, d_tile)
                 turned = tt[pl.ds(pl.multiple_of(j * share + i * d_tile, d_tile), d_tile), :]
                 part_gu[l, which, j, at] = dot(turned, src[...]).astype(BF16)
 
             tiles(share // d_tile, body)
-
-        reduce_begin(l, which, make)
+            if n == 0:
+                post_across(l, which, 0)
+                post_across(l, which, 1)
+            elif n < 3:
+                post_direct(l, which, n - 1)
 
     def reduce_pass(l, which):
         part, land, mid = views(l, which)
-        half = part.shape[1] // 2
         both = mid_dn.at[:, l] if which == 2 else mid_gu.at[:, l, which]
         wait_landed(both, mid_recv.at[3 * l + which])
-        for to, side, start in ((right, 0, 0), (left, 1, half)):
-            step = half // 4
+        for side, to in enumerate((right, left)):
+            mine, passed = half(part.at[to], which, side), mid(side)
 
             def body(i):
-                at = pl.ds(pl.multiple_of(start + i * step, step), step)
-                part[to, at] = (
-                    part[to, at].astype(F32) + mid(side)[span(i, step)].astype(F32)
-                ).astype(BF16)
+                at = span(i, mine.shape[0] // 4)
+                mine[at, :] = (mine[at, :].astype(F32) + passed[at, :].astype(F32)).astype(BF16)
 
             tiles(4, body)
-            mine = pl.ds(start, half)
-            post(l, which, part.at[to, mine], land(side).at[mine], land_recv, to)
+            post(l, which, mine, half(land(side), which, side), land_recv, to)
 
     def landing(l, which, side):
         if which == 2:
@@ -311,17 +330,21 @@
         tiles(4, body)
         total_out(l, which).start()
 
-    def load_back(i):
-        return pltpu.make_async_copy(back.at[i], recv.at[i], load_sem.at[i])
+    def load_back(i, cols, n=0):
+        return pltpu.make_async_copy(back.at[i, :, cols], recv.at[i, :, cols], load_sem.at[i + n])
+
+    def back_landed(i):
+        wait_landed(back.at[i], back_recv.at[i])
+        load_back(i, everything).start()
 
     def combine_out(l):
         i = 2 * l
-        load_back(i).wait()
-        prob = pslot[l]
         hit = sel[l].astype(F32)
-        weight = (hit * prob).T
+        weight = (hit * pslot[l]).T
         hi = weight.astype(BF16)
         lo = (weight - hi.astype(F32)).astype(BF16)
+        back_landed(i)
+        load_back(i, everything).wait()
 
         def body(n):
             cols = span(n, d_tile)
@@ -342,28 +365,44 @@
             else:
                 gg_ref[k : k + 1, :] = gg_ref[k : k + 1, :] + value
 
-    def combine_grad(l):
-        i = 2 * l + 1
-        load_back(i).wait()
+    def combine_grad_first():
+        hit = sel[0].astype(F32).T.astype(BF16)
+        back_landed(1)
+        load_back(1, everything).wait()
 
         def body(n):
             cols = span(n, d_tile)
-            value = dot(sel_t[l], recv[i, :, cols])
-            if l == 0:
-                acc[1, :, cols] = value
-            else:
-                tg_ref[:, cols] = (acc[1, :, cols] + value).astype(BF16)
+            acc[1, :, cols] = dot(hit, recv[1, :, cols])
         tiles(n_d, body)
 
+    def send_back_last():
+        for n in range(n_dp):
+            exchange(3, back, span(n, share), back_send.at[3], last_recv.at[n])
+
+    def combine_grad_last(n, hit):
+        copy = load_back(3, span(n, share), n)
+        wait_landed(back.at[3, :, span(n, share)], last_recv.at[n])
+        copy.start()
+        copy.wait()
+
+        def body(m):
+            cols = pl.ds(pl.multiple_of(n * share + m * d_tile, d_tile), d_tile)
+            tg_ref[:, cols] = (acc[1, :, cols] + dot(hit, recv[3, :, cols])).astype(BF16)
+        tiles(share // d_tile, body)
+
+    halves = (pl.ds(0, feats // 2), pl.ds(feats // 2, feats // 2))
     route(0)
-    fill_tokens(0)
+    fill_tokens(0, 0)
     pl.semaphore_wait(barrier, n_exp - 1 + 2)
-    send_tokens(0)
+    send_tokens(0, halves[0])
+    fill_tokens(0, 1)
+    send_tokens(0, halves[1])
     fill_delta(0)
     send_delta(0)
     route(1)
-    fill_tokens(1)
-    send_tokens(1)
+    fill_tokens(1, 0)
+    fill_tokens(1, 1)
+    send_tokens(1, everything)
     fill_delta(1)
     send_delta(1)
 
@@ -371,12 +410,11 @@
         copy.wait()
     tokens_landed(0)
     forward(0)
-    down_part(0)
-    turn_tokens(0)
-    reduce_pass(0, 2)
+    down_part(0, lambda: turn_tokens(0), lambda: reduce_pass(0, 2))
     deltas(0)
     gate_up_part(0, 0)
     gate_up_part(0, 1)
+    make_down(0, own)
     wait_sent(0, disp_send)
     outputs(0)
     send_back(0)
@@ -396,40 +434,34 @@
     outputs(1)
     send_back(2)
     reduce_pass(0, 1)
-    down_part(1)
+    down_part(1, lambda: None, lambda: None)
     deltas(1)
     gate_up_part(1, 0)
     gate_up_part(1, 1)
+    total_out(1, 1).start()
+    make_down(1, own)
     wait_sent(3, disp_send)
     input_grads(1)
-    send_back(3)
-
-    reduce_fetch(0, 2)
-    reduce_end(0, 2)
-    reduce_fetch(0, 0)
-    reduce_fetch(0, 1)
-    wait_landed(back.at[0], back_recv.at[0])
-    load_back(0).start()
-    reduce_end(0, 0)
-    reduce_end(0, 1)
+    send_back_last()
+
+    for which in (2, 0, 1):
+        reduce_fetch(0, which)
+        reduce_end(0, which)
     combine_out(0)
     reduce_pass(1, 2)
-    wait_landed(back.at[1], back_recv.at[1])
-    load_back(1).start()
-    combine_grad(0)
+    combine_grad_first()
     reduce_pass(1, 0)
     reduce_pass(1, 1)
-    wait_landed(back.at[2], back_recv.at[2])
-    load_back(2).start()
     combine_out(1)
-    for which in (2, 0):
-        reduce_fetch(1, which)
-        reduce_end(1, which)
-    wait_landed(back.at[3], back_recv.at[3])
-    load_back(3).start()
-    reduce_fetch(1, 1)
-    combine_grad(1)
-    reduce_end(1, 1)
+    reduce_fetch(1, 2)
+    reduce_end(1, 2)
+    hit = sel[1].astype(F32).T.astype(BF16)
+    for n in range(n_dp - 1):
+        combine_grad_last(n, hit)
+    reduce_fetch(1, 0)
+    reduce_end(1, 0)
+    combine_grad_last(n_dp - 1, hit)
+    wait_landed(land_gu.at[:, 1, 1], land_recv.at[4])
 
     for i in range(4):
         wait_sent(i, back_send)
@@ -438,6 +470,58 @@
             three = part_dn.at[l, pl.ds(0, 3)] if which == 2 else part_gu.at[l, which, pl.ds(0, 3)]
             wait_landed(three, rs_send.at[3 * l + which])
             total_out(l, which).wait()
+
+
+def finish(
+    lo_ref, tg_ref, gg_ref, gu_ref, land_ref, dn_ref,
+    lo_out, tg_out, gg_out, gate_out, up_out, down_out,
+    gu, land, dn, gate, up, down, lo, tg, gg, in_sem, out_sem, pass_sem,
+):
+    ins = [
+        pltpu.make_async_copy(src, dst, in_sem.at[n])
+        for n, (src, dst) in enumerate((
+            (gu_ref.at[0, 0], gu.at[0, 0]), (gu_ref.at[0, 1], gu.at[0, 1]),
+            (dn_ref.at[0], dn.at[0]), (dn_ref.at[1], dn.at[1]), (gu_ref.at[1, 0], gu.at[1, 0]),
+            (gu_ref.at[1, 1], gu.at[1, 1]), (land_ref.at[0, 1, 1], land.at[0]), (land_ref.at[1, 1, 1], land.at[1]),
+        ))
+    ]
+    for copy in ins:
+        copy.start()
+    rest = ((lo_ref, lo, lo_out), (tg_ref, tg, tg_out), (gg_ref, gg, gg_out))
+    entering = [pltpu.make_async_copy(src, mid, pass_sem.at[0, n]) for n, (src, mid, _) in enumerate(rest)]
+    through = [pltpu.make_async_copy(mid, dst, pass_sem.at[1, n]) for n, (_, mid, dst) in enumerate(rest)]
+    for copy in entering:
+        copy.start()
+    work = (
+        (ins[:1], (gu.at[0, 0],), gate.at[0], gate_out.at[0]),
+        (ins[1:2], (gu.at[0, 1],), gate.at[1], gate_out.at[1]),
+        (ins[2:3], (dn.at[0],), down.at[0], down_out.at[0]),
+        (ins[3:4], (dn.at[1],), down.at[1], down_out.at[1]),
+        (ins[4:5], (gu.at[1, 0],), up.at[0], up_out.at[0]),
+        (ins[5:], (gu.at[1, 1], land.at[0], land.at[1]), up.at[1], up_out.at[1]),
+    )
+    outs = []
+    for n, (needs, terms, made, dst) in enumerate(work):
+        for copy in needs:
+            copy.wait()
+        step = made.shape[0] // 8
+
+        def body(i):
+            at = span(i, step)
+            total = terms[0][at, :].astype(F32)
+            for term in terms[1:]:
+                total = total + term[at, :].astype(F32)
+            made[at, :] = total
+
+        tiles(8, body)
+        outs.append(pltpu.make_async_copy(made, dst, out_sem.at[n]))
+        outs[-1].start()
+    for copy in entering:
+        copy.wait()
+    for copy in through:
+        copy.start()
+    for copy in through + outs:
+        copy.wait()
 
 
 def shards(n_dp, n_exp, tokens, expert_ids, gate_probs, w_gate, w_up, w_down, out_grad):
@@ -479,22 +563,22 @@
             pltpu.VMEM((2, 2, n_dp, share, hidden), BF16),
             pltpu.VMEM((2, n_dp, hidden, share), BF16),
             pltpu.VMEM((2, 2, 2, share // 2, hidden), BF16),
-            pltpu.VMEM((2, 2, hidden // 2, share), BF16),
+            pltpu.VMEM((2, 2, hidden, share // 2), BF16),
             pltpu.VMEM((2, rows, tok), BF16),
-            pltpu.VMEM((2, tok, rows), BF16),
             pltpu.VMEM((2, rows, 1), F32),
             pltpu.VMEM((2, tok, feats), F32),
             pltpu.SemaphoreType.DMA((3,)),
             pltpu.SemaphoreType.DMA((4,)),
             pltpu.SemaphoreType.DMA((2,)),
-            pltpu.SemaphoreType.DMA((2, 4)),
+            pltpu.SemaphoreType.DMA((2, 7)),
             pltpu.SemaphoreType.DMA((4,)),
+            pltpu.SemaphoreType.DMA((3,)),
             pltpu.SemaphoreType.DMA((4,)),
             pltpu.SemaphoreType.DMA((6,)),
             pltpu.SemaphoreType.DMA((6,)),
             pltpu.SemaphoreType.DMA((6,)),
             pltpu.SemaphoreType.DMA((6, 3)),
-            pltpu.SemaphoreType.DMA((4,)),
+            pltpu.SemaphoreType.DMA((7,)),
         ],
         compiler_params=pltpu.CompilerParams(
             collective_id=0, has_side_effects=True, vmem_limit_bytes=62 * 2**20
@@ -503,8 +587,36 @@
             flops=18 * 2 * rows * feats * hidden, bytes_accessed=60_000_000, transcendentals=4 * rows * hidden
         ),
     )(expert_ids.T, gate_probs.T, tokens, out_grad, w_gate, w_up, w_down)
-    layer_out, token_grad, gate_grad, sum_gu, sum_dn, *_ = outs
-    return layer_out, token_grad, gate_grad.T, sum_gu[0].astype(F32), sum_gu[1].astype(F32), sum_dn.astype(F32)
+    layer_out, token_grad, gate_grad, sum_gu, sum_dn, land_gu, *_ = outs
+    layer_out, token_grad, gate_grad, grad_gate, grad_up, grad_down = pl.pallas_call(
+        finish,
+        out_shape=[
+            shape((tok, feats), BF16),
+            shape((tok, feats), BF16),
+            shape((top, tok), F32),
+            shape((2, share, hidden), F32),
+            shape((2, share, hidden), F32),
+            shape((2, hidden, share), F32),
+        ],
+        in_specs=[far] * 6,
+        out_specs=[far] * 6,
+        scratch_shapes=[
+            pltpu.VMEM((2, 2, share, hidden), BF16),
+            pltpu.VMEM((2, share, hidden), BF16),
+            pltpu.VMEM((2, hidden, share), BF16),
+            pltpu.VMEM((2, share, hidden), F32),
+            pltpu.VMEM((2, share, hidden), F32),
+            pltpu.VMEM((2, hidden, share), F32),
+            pltpu.VMEM((tok, feats), BF16),
+            pltpu.VMEM((tok, feats), BF16),
+            pltpu.VMEM((top, tok), F32),
+            pltpu.SemaphoreType.DMA((8,)),
+            pltpu.SemaphoreType.DMA((6,)),
+            pltpu.SemaphoreType.DMA((2, 3)),
+        ],
+        compiler_params=pltpu.CompilerParams(vmem_limit_bytes=62 * 2**20),
+    )(layer_out, token_grad, gate_grad, sum_gu, land_gu, sum_dn)
+    return layer_out, token_grad, gate_grad.T, grad_gate, grad_up, grad_down
 
 
 def solution(mesh):

time: 214 us -> 208 us (0.972)
  other arithmetic: 6.91 us -> 0 us
  Pallas kernels: 204 us -> 207 us
  local copies, waits for them, and re-layouts: 2.18 us -> 0 us
    pallas_call x0 -> x1, Pallas kernels: none -> 7.25 us  [shards(): pl.pallas_call(finish, out_shape=[shape((tok, feats), BF16), shape((tok,...]
    convert_element_type x2 -> x0, other arithmetic: 6.91 us -> none  [the longest x1 3.67 us: shards(): sum_dn.astype(F32)]
    pallas_call x1, Pallas kernels: 204 us -> 200 us  [shards(): pl.pallas_call(functools.partial(kernel, n_dp, n_exp), out_shape=[shape((...]
    unnamed x11 -> x0, local copies, waits for them, and re-layouts: 2.18 us -> none
where the time goes in v3:
time: 208 us
  Pallas kernels  207 us (100%)
    pallas_call x1, Pallas kernels, shards(): pl.pallas_call(functools.partial(kernel, n_dp, n_exp), out_shape=[shape((...  200 us
    pallas_call x1, Pallas kernels, shards(): pl.pallas_call(finish, out_shape=[shape((tok, feats), BF16), shape((tok,...  7.25 us

profile of v3, /device:TPU:1, one launch (start us, length us, event | category | flops | bytes accessed | tf_op | source)
XLA Modules:
  0.0 207.6 jit_solution(18154480266717163064)
XLA Ops:
  0.6 199.6 %shard_map.118 = (bf16[128,2048]{1,0:T(8,128)(2,1)}, bf16[128,2048]{1,0:T(8,128)(2,1)}, f32[4,128]{1,0:T(4,128)}, bf16[2,2,512,768]{3,2,1,0:T(8,128)(2,1)}, bf16...) custom-call(s32[4,128]{1,0:T(4,128)} %bitcast.3, ...), custom_call_target="tpu_custom_call" | custom-call | flops 28991029248 | bytes 60000000 | tf_op jit(solution)/shard_map/pallas_call | solution.py:536
  200.2 7.3 %shard_map.119 = (bf16[128,2048]{1,0:T(8,128)(2,1)}, bf16[128,2048]{1,0:T(8,128)(2,1)}, f32[4,128]{1,0:T(4,128)}, f32[2,512,768]{2,1,0:T(8,128)}, f32[2,512,768]{2,1,0:T(8,128)}, /*index=5*/f32[2,768,512]{2,1,0:T(8,128)}) custom-call(bf16[128,2048]{1,0:T(8,128)(2,1)} %get-tuple-element.18.lo_ref, bf16[128,2048]{1,0:T(8,128)(2,1)} %get-tuple-element.19.tg_ref, ...), custom_call_target="tpu_custom_call" | custom-call | tf_op jit(solution)/shard_map/pallas_call | solution.py:591

commit v4 on v3

--- a/solution.py
+++ b/solution.py
@@ -32,11 +32,11 @@
 
 def kernel(
     n_dp, n_exp,
-    ids_ref, probs_ref, tok_ref, og_ref, wg_hbm, wu_hbm, wd_hbm,
+    ids_ref, probs_ref, tok_hbm, og_hbm, wg_hbm, wu_hbm, wd_hbm,
     lo_ref, tg_ref, gg_ref, sum_gu, sum_dn, land_gu, land_dn, back,
-    send, recv, tt, wg, wu, wd, act, act_t, gd, ud, pre_g, pre_u,
+    tok_ref, og_ref, send, recv, tt, wg, wu, wd, act, act_t, gd, ud, pre_g, pre_u,
     part_gu, part_dn, mid_gu, mid_dn, sel, pslot, acc,
-    w_sem, disp_send, tok_recv, delta_recv, back_send, back_recv, last_recv,
+    in_sem, w_sem, disp_send, tok_recv, delta_recv, back_send, back_recv, last_recv,
     rs_send, mid_recv, land_recv, sum_sem, load_sem,
 ):
     dp, me = lax.axis_index("dp"), lax.axis_index("expert")
@@ -60,6 +60,13 @@
         c = lax.rem(c + lax.rem(off, 2), 2)
         return (z * 4 + y) * 2 + c
 
+    rows_in = [
+        pltpu.make_async_copy(src, dst, in_sem.at[i])
+        for i, (src, dst) in enumerate(((tok_hbm, tok_ref), (og_hbm, og_ref)))
+    ]
+    for copy in rows_in:
+        copy.start()
+
     barrier = pltpu.get_barrier_semaphore()
 
     def greet(k, carry):
@@ -75,9 +82,6 @@
             pltpu.make_async_copy(src.at[l], dst, w_sem.at[i])
             for i, (src, dst) in enumerate(((wg_hbm, wg), (wu_hbm, wu), (wd_hbm, wd)))
         ]
-
-    for copy in weights(0):
-        copy.start()
 
     ids_t, probs_t = ids_ref[...], probs_ref[...]
     earlier = (
@@ -392,11 +396,15 @@
 
     halves = (pl.ds(0, feats // 2), pl.ds(feats // 2, feats // 2))
     route(0)
+    rows_in[0].wait()
     fill_tokens(0, 0)
     pl.semaphore_wait(barrier, n_exp - 1 + 2)
     send_tokens(0, halves[0])
     fill_tokens(0, 1)
     send_tokens(0, halves[1])
+    rows_in[1].wait()
+    for copy in weights(0):
+        copy.start()
     fill_delta(0)
     send_delta(0)
     route(1)
@@ -545,9 +553,11 @@
             shape((2, 2, hidden, share), BF16),
             shape((4, rows, feats), BF16),
         ],
-        in_specs=[vmem] * 4 + [far] * 3,
+        in_specs=[vmem] * 2 + [far] * 5,
         out_specs=[vmem] * 3 + [far] * 5,
         scratch_shapes=[
+            pltpu.VMEM((tok, feats), BF16),
+            pltpu.VMEM((tok, feats), BF16),
             pltpu.VMEM((4, rows, feats), BF16),
             pltpu.VMEM((4, rows, feats), BF16),
             pltpu.VMEM((feats, rows), BF16),
@@ -567,6 +577,7 @@
             pltpu.VMEM((2, rows, tok), BF16),
             pltpu.VMEM((2, rows, 1), F32),
             pltpu.VMEM((2, tok, feats), F32),
+            pltpu.SemaphoreType.DMA((2,)),
             pltpu.SemaphoreType.DMA((3,)),
             pltpu.SemaphoreType.DMA((4,)),
             pltpu.SemaphoreType.DMA((2,)),

time: 208 us -> 208 us (level)
  no operation moved by 1% of the time
where the time goes in v4:
time: 208 us
  Pallas kernels  207 us (100%)
    pallas_call x1, Pallas kernels, shards(): pl.pallas_call(functools.partial(kernel, n_dp, n_exp), out_shape=[shape((...  200 us
    pallas_call x1, Pallas kernels, shards(): pl.pallas_call(finish, out_shape=[shape((tok, feats), BF16), shape((tok,...  7.25 us

profile of v4, /device:TPU:1, one launch (start us, length us, event | category | flops | bytes accessed | tf_op | source)
XLA Modules:
  0.0 207.7 jit_solution(14996875906333863320)
XLA Ops:
  0.6 199.6 %shard_map.118 = (bf16[128,2048]{1,0:T(8,128)(2,1)}, bf16[128,2048]{1,0:T(8,128)(2,1)}, f32[4,128]{1,0:T(4,128)}, bf16[2,2,512,768]{3,2,1,0:T(8,128)(2,1)}, bf16...) custom-call(s32[4,128]{1,0:T(4,128)} %bitcast.3, ...), custom_call_target="tpu_custom_call" | custom-call | flops 28991029248 | bytes 60000000 | tf_op jit(solution)/shard_map/pallas_call | solution.py:544
  200.3 7.3 %shard_map.119 = (bf16[128,2048]{1,0:T(8,128)(2,1)}, bf16[128,2048]{1,0:T(8,128)(2,1)}, f32[4,128]{1,0:T(4,128)}, f32[2,512,768]{2,1,0:T(8,128)}, f32[2,512,768]{2,1,0:T(8,128)}, /*index=5*/f32[2,768,512]{2,1,0:T(8,128)}) custom-call(bf16[128,2048]{1,0:T(8,128)(2,1)} %get-tuple-element.18.lo_ref, bf16[128,2048]{1,0:T(8,128)(2,1)} %get-tuple-element.19.tg_ref, ...), custom_call_target="tpu_custom_call" | custom-call | tf_op jit(solution)/shard_map/pallas_call | solution.py:602
